TPU v7x, 512 devices: a whole 4x4x16 slice. The times are simulated.
512 devices in a mesh: ctx: 128 (over y, z, core), ch: 4 (over x).
Axes of the slice: x: 4, y: 4, z: 16, core: 2. Of those that a mesh axis runs over, the one named last changes fastest.
Arguments:
- projections: bfloat16 [3, 32768, 1024], P(None, 'ctx', 'ch'), may hold values from -6 to 6
- filtered: bfloat16 [32768, 1024], P('ctx', 'ch'), may hold values from -6 to 6
- cotangent: bfloat16 [32768, 1024], P('ctx', 'ch'), may hold values from -9 to 9
- short_taps: float32 [3, 3, 1024], P(None, None, 'ch'), may hold values from -3.5 to 3.5
- residues: float32 [1024, 16], P('ch'), may hold values from -1.5 to 1.5
- pole_rates: float32 [1024, 16], P('ch'), may hold values from 0.5 to 1092.2667
- skip_gain: float32 [1024], P('ch'), may hold values from -4 to 4
Outputs:
- grad_projections: bfloat16 [3, 32768, 1024], P(None, 'ctx', 'ch')
- grad_short: float32 [3, 3, 1024], P(None, None, 'ch')
- grad_residues: float32 [1024, 16], P('ch')
- grad_rates: float32 [1024, 16], P('ch')
- grad_skip: float32 [1024], P('ch')
All inputs are finite; a program needn't handle non-finite values.
Results may differ from a plain program's by a relative error of at most 0.013.
Values may be sent and summed in bfloat16 or wider, within the bound.
A program may use at most 64 MiB of HBM per device.

v0:
```python
import math

import jax
import jax.numpy as jnp
from jax import lax
from jax.sharding import PartitionSpec as P

highest = lax.Precision.HIGHEST


def from_behind(block, axis, distance):
    devices = range(lax.axis_size(axis))
    route = [(i - distance, i) for i in devices if i - distance in devices]
    return lax.ppermute(block, axis, route)


def twiddle_table(left_index, right_index, period, direction):
    phases = (left_index * right_index % period).astype(jnp.float32) * (2.0 * math.pi / period)
    return (jnp.cos(phases), direction * jnp.sin(phases))


def apply_complex(formula, matrix_real, matrix_imag, data_real, data_imag):
    out_real = jnp.einsum(formula, matrix_real, data_real, precision=highest) - jnp.einsum(
        formula, matrix_imag, data_imag, precision=highest
    )
    out_imag = jnp.einsum(formula, matrix_real, data_imag, precision=highest) + jnp.einsum(
        formula, matrix_imag, data_real, precision=highest
    )
    return (out_real, out_imag)


def times_complex(left_real, left_imag, right_real, right_imag):
    return (
        left_real * right_real - left_imag * right_imag,
        left_real * right_imag + left_imag * right_real,
    )


def rows_to_spectrum(data_real, data_imag, groups, sub_rows):
    row_count = groups * sub_rows
    freq_index = jnp.arange(row_count, dtype=jnp.int32)[:, None, None]
    row_index = (
        jnp.arange(groups, dtype=jnp.int32)[:, None] * sub_rows
        + jnp.arange(sub_rows, dtype=jnp.int32)[None, :]
    )[None, :, :]
    matrix_real, matrix_imag = twiddle_table(freq_index, row_index, row_count, -1.0)
    return apply_complex("fqr,qasrc->asfc", matrix_real, matrix_imag, data_real, data_imag)


def spectrum_to_rows(spec_real, spec_imag, groups, sub_rows):
    row_count = groups * sub_rows
    freq_index = jnp.arange(row_count, dtype=jnp.int32)[:, None, None]
    row_index = (
        jnp.arange(groups, dtype=jnp.int32)[:, None] * sub_rows
        + jnp.arange(sub_rows, dtype=jnp.int32)[None, :]
    )[None, :, :]
    matrix_real, matrix_imag = twiddle_table(freq_index, row_index, row_count, 1.0)
    return apply_complex("fqr,asfc->qasrc", matrix_real, matrix_imag, spec_real, spec_imag)


def seq_transpose(blocks):
    return lax.all_to_all(blocks, "ctx", split_axis=0, concat_axis=0, tiled=True)


def freq_transpose(blocks):
    return lax.all_to_all(
        blocks.astype(jnp.bfloat16), "ctx", split_axis=0, concat_axis=0, tiled=True
    ).astype(blocks.dtype)


def body(projections, filtered, cotangent, short_taps, residues, pole_rates, skip_gain):
    groups = lax.axis_size("ctx")
    own_index = lax.axis_index("ctx")
    tap_count = short_taps.shape[1]
    row_count = projections.shape[1]
    channels = projections.shape[2]
    sub_rows = row_count // groups
    tokens = row_count * groups
    spectrum_size = 2 * tokens
    prev_rim = from_behind(projections[:, row_count - (tap_count - 1) :, :], "ctx", 1)
    extended = jnp.concatenate([prev_rim, projections], axis=1).astype(jnp.float32)
    features = jnp.zeros((3, row_count, channels), jnp.float32)
    for tap_index in range(tap_count):
        lead_rows = tap_count - 1 - tap_index
        features = (
            features
            + short_taps[:, tap_index, None, :] * extended[:, lead_rows : lead_rows + row_count, :]
        )
    query_feat = features[0]
    key_feat = features[1]
    value_feat = features[2]
    upstream = cotangent.astype(jnp.float32)
    grad_filtered = upstream * query_feat
    grad_query = upstream * filtered.astype(jnp.float32)
    gated_value = key_feat * value_feat
    outgoing = jnp.stack(
        [
            grad_filtered.reshape(groups, sub_rows, channels),
            gated_value.reshape(groups, sub_rows, channels),
        ],
        axis=1,
    )
    incoming = seq_transpose(outgoing)
    group_index = jnp.arange(groups, dtype=jnp.int32)[:, None]
    slot_index = jnp.arange(2, dtype=jnp.int32)[None, :]
    freq_order = jnp.where(
        slot_index == 0, group_index, jnp.where(group_index == 0, groups, 2 * groups - group_index)
    )
    first_real, first_imag = twiddle_table(
        freq_order.reshape(2 * groups)[:, None],
        jnp.arange(groups, dtype=jnp.int32)[None, :],
        2 * groups,
        -1.0,
    )
    section_real = jnp.einsum("fj,jsrc->fsrc", first_real, incoming, precision=highest)
    section_imag = jnp.einsum("fj,jsrc->fsrc", first_imag, incoming, precision=highest)
    signals = section_real.shape[1]
    section_real = section_real.reshape(groups, 2, signals, sub_rows, channels)
    section_imag = section_imag.reshape(groups, 2, signals, sub_rows, channels)
    own_rows = own_index * sub_rows + jnp.arange(sub_rows, dtype=jnp.int32)
    turn_real, turn_imag = twiddle_table(
        freq_order[:, :, None], own_rows[None, None, :], spectrum_size, -1.0
    )
    section_real, section_imag = times_complex(
        section_real, section_imag, turn_real[:, :, None, :, None], turn_imag[:, :, None, :, None]
    )
    arrived = freq_transpose(jnp.stack([section_real, section_imag], axis=2))
    spec_real, spec_imag = rows_to_spectrum(arrived[:, :, 0], arrived[:, :, 1], groups, sub_rows)
    grad_real = spec_real[:, 0]
    grad_imag = spec_imag[:, 0]
    gated_real = spec_real[:, 1]
    gated_imag = spec_imag[:, 1]
    own_order = jnp.stack([own_index, jnp.where(own_index == 0, groups, 2 * groups - own_index)])
    freq_values = own_order[:, None] + 2 * groups * jnp.arange(row_count, dtype=jnp.int32)[None, :]
    phases = freq_values.astype(jnp.float32) * (2.0 * math.pi / spectrum_size)
    cos_phase = jnp.cos(phases)[:, :, None]
    sin_phase = jnp.sin(phases)[:, :, None]
    half_sine = jnp.sin(0.5 * phases)[:, :, None]
    one_minus = 2.0 * half_sine * half_sine
    parity = (1 - 2 * (own_order % 2)).astype(jnp.float32)[:, None, None]
    cross_real = grad_real * gated_real + grad_imag * gated_imag
    cross_imag = grad_imag * gated_real - grad_real * gated_imag

    def one_mode(carried, params):
        residue, rate_value = params
        per_token = rate_value / tokens
        per_step = jnp.exp(-per_token)
        root_decay = jnp.sqrt(per_token)
        far_tail = jnp.exp(-rate_value)
        den_real = -jnp.expm1(-per_token) + per_step * one_minus
        den_imag = per_step * sin_phase
        den_norm = den_real * den_real + den_imag * den_imag
        numerator = 1.0 - far_tail * parity
        base_real = numerator * den_real / den_norm
        base_imag = -numerator * den_imag / den_norm
        filter_real = carried[0] + residue * root_decay * base_real
        filter_imag = carried[1] + residue * root_decay * base_imag
        residue_term = (
            jnp.sum(cross_real * base_real + cross_imag * base_imag, axis=(0, 1)) * root_decay
        )
        turned_real = per_step * (base_real * cos_phase + base_imag * sin_phase)
        turned_imag = per_step * (base_imag * cos_phase - base_real * sin_phase)
        lead_real = far_tail * parity - turned_real / tokens
        lead_imag = -turned_imag / tokens
        quot_real = (lead_real * den_real + lead_imag * den_imag) / den_norm
        quot_imag = (lead_imag * den_real - lead_real * den_imag) / den_norm
        slope_real = base_real * (0.5 / rate_value) + quot_real
        slope_imag = base_imag * (0.5 / rate_value) + quot_imag
        rate_term = jnp.sum(cross_real * slope_real + cross_imag * slope_imag, axis=(0, 1)) * (
            residue * root_decay
        )
        return ((filter_real, filter_imag), (residue_term, rate_term))

    zero_field = jnp.zeros((2, row_count, channels), jnp.float32)
    filter_pair, mode_terms = lax.scan(
        one_mode, (zero_field, zero_field), (residues.T, pole_rates.T)
    )
    filter_real, filter_imag = filter_pair
    residue_terms, rate_terms = mode_terms
    back_real = filter_real * grad_real + filter_imag * grad_imag
    back_imag = filter_real * grad_imag - filter_imag * grad_real
    rows_real, rows_imag = spectrum_to_rows(
        back_real[:, None], back_imag[:, None], groups, sub_rows
    )
    block_rows = (
        jnp.arange(groups, dtype=jnp.int32)[:, None] * sub_rows
        + jnp.arange(sub_rows, dtype=jnp.int32)[None, :]
    )
    undo_real, undo_imag = twiddle_table(
        own_order[None, :, None], block_rows[:, None, :], spectrum_size, 1.0
    )
    rows_real, rows_imag = times_complex(
        rows_real, rows_imag, undo_real[:, :, None, :, None], undo_imag[:, :, None, :, None]
    )
    returned = freq_transpose(jnp.stack([rows_real, rows_imag], axis=2))
    last_real = returned[:, :, 0].reshape(2 * groups, 1, sub_rows, channels)
    last_imag = returned[:, :, 1].reshape(2 * groups, 1, sub_rows, channels)
    sequence_part = jnp.einsum(
        "fj,fsrc->jsrc", first_real, last_real, precision=highest
    ) + jnp.einsum("fj,fsrc->jsrc", first_imag, last_imag, precision=highest)
    long_part = seq_transpose(sequence_part).reshape(row_count, channels) / spectrum_size
    residue_owned = residue_terms.T / spectrum_size
    rate_owned = rate_terms.T / spectrum_size
    grad_gated = long_part + skip_gain * grad_filtered
    grad_stack = jnp.stack([grad_query, grad_gated * value_feat, grad_gated * key_feat])
    next_rim = from_behind(grad_stack[:, : tap_count - 1, :], "ctx", -1)
    grads_ext = jnp.concatenate([grad_stack, next_rim], axis=1)
    grad_proj = jnp.zeros_like(grad_stack)
    tap_terms = []
    for tap_index in range(tap_count):
        grad_proj = (
            grad_proj
            + short_taps[:, tap_index, None, :] * grads_ext[:, tap_index : tap_index + row_count, :]
        )
        lead_rows = tap_count - 1 - tap_index
        tap_terms.append(
            jnp.sum(grad_stack * extended[:, lead_rows : lead_rows + row_count, :], axis=1)
        )
    skip_term = jnp.sum(grad_filtered * gated_value, axis=0)
    residue_sum, rate_sum, skip_sum, tap_sum = lax.psum(
        (residue_owned, rate_owned, skip_term, jnp.stack(tap_terms, axis=1)), "ctx"
    )
    token_scale = 1.0 / math.sqrt(tokens)
    return (
        grad_proj.astype(jnp.bfloat16),
        tap_sum * token_scale,
        residue_sum * token_scale,
        rate_sum * token_scale,
        skip_sum * token_scale,
    )


def solution(mesh):
    placed = (
        P(None, "ctx", "ch"),
        P("ctx", "ch"),
        P("ctx", "ch"),
        P(None, None, "ch"),
        P("ch", None),
        P("ch", None),
        P("ch"),
    )
    return jax.shard_map(
        body,
        mesh=mesh,
        in_specs=placed,
        out_specs=(
            P(None, "ctx", "ch"),
            P(None, None, "ch"),
            P("ch", None),
            P("ch", None),
            P("ch"),
        ),
        check_vma=False,
    )
```

profile of v0, /device:TPU:1, one launch (start us, length us, event | category | flops | bytes accessed | tf_op | source)
XLA Modules:
  0.0 782.2 jit_solution(8210581733760482657)
XLA Ops:
  1.3 4.9 collective-permute-start
  6.3 0.8 fusion.168
  7.1 3.0 collective-permute-done
  10.1 1.1 maximum_convert_fusion
  11.5 1.0 copy-done.8
  13.4 1.0 copy.105
  14.4 17.9 %all-to-all-start = ((f32[128,2,2,256]{3,2,1,0:T(2,128)}), f32[128,2,2,256]{3,2,1,0:T(2,128)S(1)}, u32[]{:S(2)}, u32[]{:S(2)}) async-start(f32[128,2,2,256]{3,2,1,0:T(2,128)} %copy.105), calls=%async_computation | async-start | bytes 1048576 | tf_op jit(solution)/shard_map/all_to_all | solution.py:62
  32.7 32.7 %all-to-all-done = f32[128,2,2,256]{3,2,1,0:T(2,128)S(1)} async-done(((f32[128,2,2,256]{3,2,1,0:T(2,128)}), f32[128,2,2,256]{3,2,1,0:T(2,128)S(1)}, u32[]{:S(2)}, u32[]{:S(2)}) %all-to-all-start) | async-done | bytes 524320 | tf_op jit(solution)/shard_map/all_to_all | solution.py:62
  65.5 1.5 fusion.41
  67.0 0.8 copy.113
  67.8 1.5 fusion.43
  69.3 0.8 copy.108
  70.9 2.1 copy.117
  72.9 7.9 %all-to-all-start.1 = ((bf16[128,2,2,2,2,256]{5,4,3,1,2,0:T(2,128)(2,1)}), bf16[128,2,2,2,2,256]{5,4,3,1,2,0:T(2,128)(2,1)}, u32[]{:S(2)}, u32[]{:S(2)}) async-start(bf16[128,2,2,2,2,256]{5,4,3,1,2,0:T(2,128)(2,1)} %copy.117), calls=%async_computation.1 | async-start | bytes 2097152 | tf_op jit(solution)/shard_map/all_to_all | solution.py:66
  81.2 53.7 %all-to-all-done.1 = bf16[128,2,2,2,2,256]{5,4,3,1,2,0:T(2,128)(2,1)} async-done(((bf16[128,2,2,2,2,256]{5,4,3,1,2,0:T(2,128)(2,1)}), bf16[128,2,2,2,2,256]{5,4,3,1,2,0:T(2,128)(2,1)}, u32[]{:S(2)}, u32[]{:S(2)}) %all-to-all-start.1) | async-done | bytes 1048608 | tf_op jit(solution)/shard_map/all_to_all | solution.py:66
  135.0 1.9 fusion.166
  136.9 1.3 copy.156
  138.1 1.2 copy.154
  139.3 1.3 copy.157
  141.1 2.7 convolution_bitcast_fusion
  143.8 1.6 convolution_bitcast_fusion.2
  145.4 1.6 fusion.24
  147.1 1.6 fusion.22
  148.7 1.1 multiply_subtract_fusion.1
  150.0 1.2 copy.124
  151.2 50.2 %while.19 = (s32[]{:T(128)}, f32[2,256,256]{2,1,0:T(8,128)S(1)}, f32[2,256,256]{2,1,0:T(8,128)S(1)}, f32[16,256]{1,0:T(8,128)S(1)}, f32[16,256]{1,0:T(8,128)S(1)...) while((s32[]{:T(128)}, f32[2,256,256]{2,1,0:T(8,128)S(1)}, ...), condition=%wide.region_3.4_spmd.clone.clone.clone, body=%wide.region_0.3_spmd.clone.clone.clone.sunk | while | flops 7608579 | bytes 3205295 | solution.py:175
  152.2 0.9 fusion.177
  153.1 0.7 fusion.178
  155.3 0.9 fusion.177
  158.4 0.9 fusion.177
  161.6 0.9 fusion.177
  162.5 0.7 fusion.178
  164.7 0.9 fusion.177
  165.6 0.7 fusion.178
  167.8 0.9 fusion.177
  171.0 0.9 fusion.177
  171.8 0.7 fusion.178
  174.1 0.9 fusion.177
  175.0 0.7 fusion.178
  177.2 0.9 fusion.177
  180.3 0.9 fusion.177
  183.5 0.9 fusion.177
  186.6 0.9 fusion.177
  189.7 0.9 fusion.177
  192.9 0.9 fusion.177
  196.0 0.9 fusion.177
  199.1 0.9 fusion.177
  201.5 1.0 copy.125
  202.5 1.0 copy.126
  203.6 1.5 multiply_add_fusion.2
  205.1 1.6 fusion.36
  206.6 1.6 fusion.34
  208.2 1.6 fusion.25
  209.7 1.7 fusion.49
  212.0 41.5 %all_to_all.20 = bf16[128,2,2,1,2,256]{5,4,1,3,2,0:T(2,128)(2,1)S(1)} all-to-all(bf16[128,2,2,1,2,256]{5,4,1,3,2,0:T(2,128)(2,1)S(1)} %copy.129), channel_id=1, replica_groups=mesh['ctx'=128,'ch'=4] {'ctx'}, dimensions={0} | all-to-all | bytes 1048576 | tf_op jit(solution)/shard_map/all_to_all | solution.py:66
  253.8 0.8 fusion.64
  254.6 0.8 fusion.27
  255.4 0.9 copy.132
  256.3 7.3 all-to-all-start.3
  263.6 22.5 %all-to-all-done.3 = f32[128,1,2,256]{3,2,1,0:T(2,128)S(1)} async-done(((f32[128,1,2,256]{3,2,1,0:T(2,128)}), f32[128,1,2,256]{3,2,1,0:T(2,128)S(1)}, u32[]{:S(2)}, u32[]{:S(2)}) %all-to-all-start.3) | async-done | bytes 262176 | tf_op jit(solution)/shard_map/all_to_all | solution.py:62
  287.0 4.0 collective-permute-start.1
  291.1 1.5 collective-permute-done.1
  292.6 1.3 multiply_reduce_fusion.2
  293.9 485.7 %all-reduce = (f32[3,3,256]{2,0,1:T(4,128)S(1)}, f32[256,16]{0,1:T(8,128)S(1)}, f32[256,16]{0,1:T(8,128)S(1)}, f32[256]{0:T(256)S(1)}) all-reduce(f32[3,3,256]{2,0,1:T(4,128)S(1)} %pad_maximum_fusion.5, f32[256,16]{0,1:T(8,128)S(1)} %multiply_bitcast_fusion.1, ...), channel_id=1, replica_groups=mesh['ctx'=128,'ch'=4] {'ctx'}, use_global_device_ids=true, to_apply=%region_7.8 | all-reduce | flops 10752 | bytes 86016 | tf_op jit(solution)/shard_map/psum | solution.py:220
  (175 shorter events, 40.1 us)
Async XLA Ops:
  1.3 8.8 %collective-permute-start = (bf16[3,2,256]{2,1,0:T(2,128)(2,1)S(1)}, bf16[3,2,256]{2,1,0:T(2,128)(2,1)S(1)}, u32[]{:S(2)}, u32[]{:S(2)}) collective-permute-start(bf16[3,2,256]{2,1,0:T(2,128)(2,1)S(1)} %slice.70), channel_id=1, source_target_pairs={{0,4},{4,8},{8,12},{12,16},{16,20},{20,24},{24,28},{28,32},{32,36}... | collective-permute-start | bytes 9224 | tf_op jit(solution)/shard_map/ppermute | solution.py:14
  11.5 1.4 copy-start
  11.5 1.0 copy-start.8
  11.5 1.2 copy-start.9
  14.4 51.1 %all-to-all-start = ((f32[128,2,2,256]{3,2,1,0:T(2,128)}), f32[128,2,2,256]{3,2,1,0:T(2,128)S(1)}, u32[]{:S(2)}, u32[]{:S(2)}) async-start(f32[128,2,2,256]{3,2,1,0:T(2,128)} %copy.105), calls=%async_computation | async-start | bytes 1048576 | tf_op jit(solution)/shard_map/all_to_all | solution.py:62
  72.9 62.0 %all-to-all-start.1 = ((bf16[128,2,2,2,2,256]{5,4,3,1,2,0:T(2,128)(2,1)}), bf16[128,2,2,2,2,256]{5,4,3,1,2,0:T(2,128)(2,1)}, u32[]{:S(2)}, u32[]{:S(2)}) async-start(bf16[128,2,2,2,2,256]{5,4,3,1,2,0:T(2,128)(2,1)} %copy.117), calls=%async_computation.1 | async-start | bytes 2097152 | tf_op jit(solution)/shard_map/all_to_all | solution.py:66
  141.1 2.7 copy-start.7
  143.8 1.6 copy-start.5
  147.0 1.6 copy-start.2
  148.7 1.1 copy-start.4
  201.5 2.0 copy-start.3
  202.5 1.1 copy-start.6
  256.3 30.1 %copy-start.1 = (f32[3,256,256]{2,1,0:T(8,128)S(1)}, f32[3,256,256]{2,1,0:T(8,128)}, u32[]{:S(2)}) copy-start(f32[3,256,256]{2,1,0:T(8,128)} %copy-done) | copy-start | bytes 2359300
  256.3 29.8 %all-to-all-start.3 = ((f32[128,1,2,256]{3,2,1,0:T(2,128)}), f32[128,1,2,256]{3,2,1,0:T(2,128)S(1)}, u32[]{:S(2)}, u32[]{:S(2)}) async-start(f32[128,1,2,256]{3,2,1,0:T(2,128)} %copy.132), calls=%async_computation.3 | async-start | bytes 524288 | tf_op jit(solution)/shard_map/all_to_all | solution.py:62
  286.2 0.7 copy-start.10
  287.0 5.6 collective-permute-start.1
where the time goes:
time: 798 us; the launch traced here: 782 us
  blocking collectives  527 us (66%)
  waiting for transfers between devices  113 us (14%)
  other arithmetic  56.9 us (7%)
  starting transfers between devices  42 us (5%)
  local copies, waits for them, and re-layouts  22.1 us (3%)
  matrix products  18.3 us (2%)
    psum x1, blocking collectives, body(): lax.psum((residue_owned, rate_owned, skip_term, jnp.stack(tap_terms, axis...  486 us
    all_to_all x2, waiting for transfers between devices, seq_transpose(): lax.all_to_all(blocks, 'ctx', split_axis=0, concat_axis=0, tiled=True)  55.2 us
    all_to_all x1, waiting for transfers between devices, freq_transpose(): lax.all_to_all(blocks.astype(jnp.bfloat16), 'ctx', split_axis=0, concat_a...  53.7 us
    all_to_all x1, blocking collectives, freq_transpose(): lax.all_to_all(blocks.astype(jnp.bfloat16), 'ctx', split_axis=0, concat_a...  41.5 us
    all_to_all x2, starting transfers between devices, seq_transpose(): lax.all_to_all(blocks, 'ctx', split_axis=0, concat_axis=0, tiled=True)  25.2 us
  transfers between devices with their start and end apart: 5, of which 5 were waited for; matrix products, arithmetic and copies ran while one was open for 0% of the time, Pallas kernels for 0%

commit v1 on v0

v1 whole, which is shorter than its diff:
```python
import functools
import math

import jax
import jax.numpy as jnp
from jax import lax
from jax.experimental import pallas as pl
from jax.experimental.pallas import tpu as pltpu
from jax.sharding import PartitionSpec as P

MESH = pl.DeviceIdType.MESH
F32 = jnp.float32
BF16 = jnp.bfloat16

RUNS = 8
MODES = 16
ROWS = 16
ROW_L, ROW_LP, ROW_V, ROW_VP, ROW_W, ROW_R, ROW_D, ROW_X = 0, 1, 2, 3, 4, 10, 11, 12
REST = 3


def up(x, by, size):
    return pltpu.roll(x, size - by, axis=0)


def suffix(state, slope, lam, length, count):
    row = lax.broadcasted_iota(jnp.int32, state.shape, 0)
    by = 1
    while by < count:
        decay = jnp.where(row < count - by, jnp.exp(lam * float(-length * by)), 0.0)
        later, later_slope = up(state, by, count), up(slope, by, count)
        slope = slope + decay * (later_slope + float(length * by) * later)
        state = state + decay * later
        by *= 2
    inside = row < count - 1
    return (
        state,
        slope,
        jnp.where(inside, up(state, 1, count), 0.0),
        jnp.where(inside, up(slope, 1, count), 0.0),
    )


def total(x):
    return jnp.sum(x, axis=0, keepdims=True)


def rest(x):
    return x - x.astype(BF16).astype(F32)


def kernel(
    geometry,
    proj_ref,
    filt_ref,
    cot_ref,
    taps_ref,
    res_ref,
    rate_ref,
    skip_ref,
    gp_ref,
    gshort_ref,
    gres_ref,
    grate_ref,
    gskip_ref,
    ext,
    feat,
    gf,
    gv,
    gq,
    ys,
    longs,
    lams,
    coefs,
    owner_lam,
    owner_coef,
    sloc,
    crosses,
    sums,
    sbuf,
    rbuf,
    flat,
    bbuf,
    bb,
    flat2,
    si_ref,
    cbuf,
    cr,
    gs,
    halo_out_prev,
    halo_out_next,
    halo_prev,
    halo_next,
    halo_send,
    halo_recv,
    a_send,
    a_recv,
    b_send,
    b_recv,
    c_send,
    c_recv,
):
    n_ctx, n_blocks = geometry
    rows = proj_ref.shape[1]
    width = proj_ref.shape[2]
    half = width // 2
    run = rows // RUNS
    tokens = rows * n_ctx
    per_block = 8
    group = 32
    me = lax.axis_index("ctx")
    y = me // (per_block * n_blocks)
    zh = (me // per_block) % n_blocks
    lo = me % per_block
    pos = y * per_block + lo

    def member(p):
        return (p // per_block) * (per_block * n_blocks) + zh * per_block + p % per_block

    def cousin(b):
        return y * (per_block * n_blocks) + b * per_block + lo

    before, after = (me + n_ctx - 1) % n_ctx, (me + 1) % n_ctx
    barrier = pltpu.get_barrier_semaphore()
    for j in range(1, group):
        pl.semaphore_signal(barrier, inc=1, device_id={"ctx": member((pos + j) % group)}, device_id_type=MESH)
    for j in range(1, n_blocks):
        pl.semaphore_signal(barrier, inc=1, device_id={"ctx": cousin((zh + j) % n_blocks)}, device_id_type=MESH)
    for d in (before, after):
        pl.semaphore_signal(barrier, inc=1, device_id={"ctx": d}, device_id_type=MESH)

    for i in range(3):
        halo_out_next[2 * i : 2 * i + 2, :] = proj_ref[i, rows - 16 :, :].astype(F32)[14:16]
        halo_out_prev[2 * i : 2 * i + 2, :] = proj_ref[i, :16, :].astype(F32)[0:2]
    halo_out_next[6:8, :] = jnp.zeros((2, width), F32)
    halo_out_prev[6:8, :] = cot_ref[:16, :].astype(F32)[0:2]
    halo_out_prev[8:10, :] = filt_ref[:16, :].astype(F32)[0:2]
    halo_out_prev[10:16, :] = jnp.zeros((6, width), F32)

    lam_t = jnp.transpose(rate_ref[...]) * (1.0 / tokens)
    coef_t = jnp.transpose(res_ref[...]) * jnp.sqrt(lam_t)
    for m in range(MODES):
        lam_m = jnp.broadcast_to(lam_t[m : m + 1, :], (RUNS, width))
        coef_m = jnp.broadcast_to(coef_t[m : m + 1, :], (RUNS, width))
        lams[m] = lam_m
        coefs[m] = coef_m
        for h in range(2):
            owner_lam[2 * m + h] = lam_m[:, h * half : (h + 1) * half]
            owner_coef[2 * m + h] = coef_m[:, h * half : (h + 1) * half]

    row = lax.broadcasted_iota(jnp.int32, (rows, rows), 0)
    col = lax.broadcasted_iota(jnp.int32, (rows, rows), 1)
    spread = jnp.where(col == run * (row % RUNS) + row // RUNS, 1.0, 0.0).astype(BF16)

    def placed(x):
        return jnp.dot(spread, x, preferred_element_type=F32)

    for i in range(3):
        ext[i, 16:, :] = placed(proj_ref[i])
    cot = placed(cot_ref[...])
    gq[...] = cot * placed(filt_ref[...])

    pl.semaphore_wait(barrier, group - 1 + n_blocks - 1 + 2)
    to_next = pltpu.make_async_remote_copy(
        halo_out_next, halo_prev, halo_send.at[0], halo_recv.at[0], device_id={"ctx": after}, device_id_type=MESH
    )
    to_prev = pltpu.make_async_remote_copy(
        halo_out_prev, halo_next, halo_send.at[1], halo_recv.at[1], device_id={"ctx": before}, device_id_type=MESH
    )
    to_next.start()
    to_prev.start()
    to_next.wait_recv()

    first = lax.broadcasted_iota(jnp.int32, (RUNS, width), 0) == 0
    has_before = jnp.where(me > 0, 1.0, 0.0)
    for i in range(3):
        for back in (2, 1):
            tail = pltpu.roll(ext[i, 16 + RUNS * (run - back) : 16 + RUNS * (run - back + 1), :], 1, axis=0)
            rim = halo_prev[2 * i + 2 - back : 2 * i + 3 - back, :] * has_before
            ext[i, 16 - 8 * back : 24 - 8 * back, :] = jnp.where(first, rim, tail)

    def tap(i, j):
        return taps_ref[i, j : j + 1, :]

    def shifted(i, j):
        return ext[i, 16 - 8 * j : 16 - 8 * j + rows, :]

    for i in range(3):
        made = tap(i, 0) * shifted(i, 0) + tap(i, 1) * shifted(i, 1) + tap(i, 2) * shifted(i, 2)
        if i == 0:
            gf[...] = cot * made
        else:
            feat[i - 1] = made
    gv[...] = feat[0] * feat[1]
    for j in range(3):
        ys[j] = feat[1] * shifted(1, j)
        ys[3 + j] = feat[0] * shifted(2, j)
    longs[...] = jnp.zeros_like(longs)
    crosses[...] = jnp.zeros_like(crosses)

    rank = lax.broadcasted_iota(jnp.int32, (RUNS, width), 0).astype(F32)

    def one_mode(m, _):
        lam = lams[m]
        coef = coefs[m]
        a = jnp.exp(-lam)
        zero = jnp.zeros((RUNS, width), F32)
        state, slope, r_sum, d_sum, v, vp = zero, zero, zero, zero, zero, zero
        w = [zero] * 6
        for step in range(run):
            low = slice(RUNS * (run - 1 - step), RUNS * (run - step))
            high = slice(RUNS * step, RUNS * (step + 1))
            slope = a * (slope + state)
            state = a * state + gf[low, :]
            longs[low, :] += coef * state
            gv_low = gv[low, :]
            r_sum = r_sum + gv_low * state
            d_sum = d_sum + gv_low * slope
            v = a * (v + gv[high, :])
            vp = a * vp + v
            for k in range(6):
                w[k] = a * (w[k] + ys[k, high, :])
        inner, inner_slope, s_loc, sp_loc = suffix(state, slope, lam, run, RUNS)
        sloc[m] = s_loc
        weight = jnp.exp(lam * (float(run) * (rank - float(RUNS - 1))))
        sums[m, ROW_L : ROW_L + 1, :] = inner[0:1, :]
        sums[m, ROW_LP : ROW_LP + 1, :] = inner_slope[0:1, :]
        sums[m, ROW_V : ROW_V + 1, :] = total(weight * v)
        sums[m, ROW_VP : ROW_VP + 1, :] = total(weight * (vp + float(run) * (float(RUNS - 1) - rank) * v))
        state_in = coef * s_loc
        for k in range(6):
            sums[m, ROW_W + k : ROW_W + k + 1, :] = total(weight * w[k])
            crosses[k] += state_in * w[k]
        pair = (total(r_sum + v * s_loc), total(d_sum + vp * s_loc + v * sp_loc))
        for at, value in zip((ROW_R, ROW_D, ROW_X), pair + (jnp.zeros((1, width), F32),)):
            sums[m, at : at + 1, :] = value
            sums[m, at + REST : at + REST + 1, :] = rest(value)
        return 0

    lax.fori_loop(0, MODES, one_mode, 0)

    skip = skip_ref[...]
    inner_gated = longs[...] + skip * gf[...]
    plain = [total(gq[...] * shifted(0, j)) for j in range(3)]
    plain += [total(inner_gated * ys[k]) + total(crosses[k]) for k in range(6)]
    plain.append(total(gf[...] * gv[...]))
    for m, value in enumerate(plain):
        sums[m, ROW_X : ROW_X + 1, :] = value
        sums[m, ROW_X + REST : ROW_X + REST + 1, :] = rest(value)
    for m in range(MODES):
        for h in range(2):
            sbuf[2 * m + h] = sums[m, :, h * half : (h + 1) * half].astype(BF16)

    own_a = pltpu.make_async_copy(sbuf.at[pos], rbuf.at[pos], a_recv)
    own_a.start()
    for j in range(1, group):
        p = (pos + j) % group
        pltpu.make_async_remote_copy(
            sbuf.at[p], rbuf.at[pos], a_send, a_recv, device_id={"ctx": member(p)}, device_id_type=MESH
        ).start()
    pltpu.make_async_copy(rbuf, rbuf, a_recv).wait()

    lam_o = owner_lam[pos]
    coef_o = owner_coef[pos]
    flat[...] = rbuf[...].astype(F32).reshape(group * ROWS, half)
    rank8 = lax.broadcasted_iota(jnp.int32, (per_block, half), 0).astype(F32)
    weight = jnp.exp(lam_o * (float(rows) * (rank8 - float(per_block - 1))))
    inside = []
    acc_r = acc_d = acc_x = jnp.zeros((per_block, half), F32)
    acc_w = [acc_r] * 6
    for b in range(4):
        base = b * per_block * ROWS

        def item(k):
            return flat[pl.ds(base + k, per_block, stride=ROWS), :]

        state, slope, v, vp = item(ROW_L), item(ROW_LP), item(ROW_V), item(ROW_VP)
        inner, inner_slope, s_int, sp_int = suffix(state, slope, lam_o, rows, per_block)
        inside.append(s_int)
        parts = [
            inner[0:1, :],
            inner_slope[0:1, :],
            total(weight * v),
            total(weight * (vp + float(rows) * (float(per_block - 1) - rank8) * v)),
        ]
        acc_r = acc_r + (item(ROW_R) + item(ROW_R + REST)) + v * s_int
        acc_d = acc_d + (item(ROW_D) + item(ROW_D + REST)) + vp * s_int + v * sp_int
        acc_x = acc_x + (item(ROW_X) + item(ROW_X + REST))
        for k in range(6):
            w_k = item(ROW_W + k)
            parts.append(total(weight * w_k))
            acc_w[k] = acc_w[k] + w_k * s_int
        for k, part in enumerate(parts):
            flat2[b * ROWS + k : b * ROWS + k + 1, :] = part
        flat2[b * ROWS + 10 : b * ROWS + ROWS, :] = jnp.zeros((ROWS - 10, half), F32)
    for k in range(6):
        value = total(acc_w[k])
        flat2[10 + k : 11 + k, :] = value
        flat2[2 * ROWS + 10 + k : 2 * ROWS + 11 + k, :] = rest(value)
    for k, acc in enumerate((acc_r, acc_d, acc_x)):
        value = total(acc)
        flat2[ROWS + 10 + k : ROWS + 11 + k, :] = value
        flat2[ROWS + 10 + REST + k : ROWS + 11 + REST + k, :] = rest(value)
    bbuf[...] = flat2[: 4 * ROWS, :].astype(BF16).reshape(4, ROWS, half)

    own_b = pltpu.make_async_copy(bbuf, bb.at[:, zh], b_recv)
    own_b.start()
    for j in range(1, n_blocks):
        pltpu.make_async_remote_copy(
            bbuf, bb.at[:, zh], b_send, b_recv, device_id={"ctx": cousin((zh + j) % n_blocks)}, device_id_type=MESH
        ).start()
    pltpu.make_async_copy(bb, bb, b_recv).wait()

    n_int = 4 * n_blocks
    flat2[...] = bb[...].astype(F32).reshape(n_int * ROWS, half)

    def item2(k):
        return flat2[pl.ds(k, n_int, stride=ROWS), :]

    lam2 = jnp.concatenate([lam_o, lam_o], axis=0)
    v, vp = item2(ROW_V), item2(ROW_VP)
    _, _, s_all, sp_all = suffix(item2(ROW_L), item2(ROW_LP), lam2, rows * per_block, n_int)
    si_ref[...] = s_all
    parts = [total(v * s_all), total(vp * s_all + v * sp_all)]
    interval = lax.broadcasted_iota(jnp.int32, (n_int, half), 0) // n_blocks
    in_1, in_0_2 = interval == 1, (interval == 0) | (interval == 2)

    def sum_1(k):
        return total(jnp.where(in_1, item2(10 + k) + item2(10 + REST + k), 0.0))

    for k in range(2):
        parts[k] = parts[k] + sum_1(k)
    for k in range(6):
        parts.append(coef_o[0:1, :] * total(item2(ROW_W + k) * s_all + jnp.where(in_0_2, item2(10 + k), 0.0)))
    parts.append(sum_1(2))
    parts += [rest(parts[0]), rest(parts[1]), rest(parts[8])]
    row16 = lax.broadcasted_iota(jnp.int32, (ROWS, half), 0)
    common = jnp.zeros((ROWS, half), F32)
    for k, part in enumerate(parts):
        common = jnp.where(row16 == 1 + k, part, common)
    for b in range(4):
        s_dev = inside[b] + weight * si_ref[pl.ds(b * n_blocks + zh, 1), :]
        s_rest = rest(s_dev)
        for i in range(per_block):
            own = jnp.where(row16 == 0, s_dev[i : i + 1, :], common)
            cbuf[b * per_block + i] = jnp.where(row16 == 13, s_rest[i : i + 1, :], own).astype(BF16)

    own_c = pltpu.make_async_copy(cbuf.at[pos], cr.at[pos], c_recv)
    own_c.start()
    for j in range(1, group):
        p = (pos + j) % group
        pltpu.make_async_remote_copy(
            cbuf.at[p], cr.at[pos], c_send, c_recv, device_id={"ctx": member(p)}, device_id_type=MESH
        ).start()

    to_prev.wait_recv()
    has_after = jnp.where(me < n_ctx - 1, 1.0, 0.0)
    ahead = halo_next[...] * has_after

    def ahead_feat(i, k):
        mine = [ext[i, 16 + RUNS * (run - 1 - b) + RUNS - 1 : 16 + RUNS * (run - b), :] for b in range(2)]
        if k == 0:
            return tap(i, 0) * ahead[2 * i : 2 * i + 1] + tap(i, 1) * mine[0] + tap(i, 2) * mine[1]
        return tap(i, 0) * ahead[2 * i + 1 : 2 * i + 2] + tap(i, 1) * ahead[2 * i : 2 * i + 1] + tap(i, 2) * mine[0]

    ahead_f = [[ahead_feat(i, k) for k in range(2)] for i in range(3)]
    ahead_gf = [ahead[6 + k : 7 + k] * ahead_f[0][k] for k in range(2)]
    ahead_gq = [ahead[6 + k : 7 + k] * ahead[8 + k : 9 + k] for k in range(2)]

    pltpu.make_async_copy(cr, cr, c_recv).wait()
    flat[...] = cr[...].astype(F32).reshape(group * ROWS, half)

    def item3(k):
        return jnp.concatenate(
            [flat[pl.ds(h * ROWS + k, MODES, stride=2 * ROWS), :] for h in range(2)], axis=1
        )

    scale = 1.0 / math.sqrt(tokens)
    s_dev = item3(0) + item3(13)
    r_tot, d_tot, x_tot = item3(1) + item3(10), item3(2) + item3(11), item3(9) + item3(12)
    root = jnp.sqrt(lam_t)
    res_t = jnp.transpose(res_ref[...])
    rate_t = jnp.transpose(rate_ref[...])
    gres_ref[...] = jnp.transpose(scale * root * r_tot)
    grate_ref[...] = jnp.transpose(scale * res_t * root * (0.5 / rate_t * r_tot - d_tot * (1.0 / tokens)))
    for j in range(3):
        gshort_ref[0, j : j + 1, :] = scale * x_tot[j : j + 1, :]
        for i in (1, 2):
            k = 3 * (i - 1) + j
            gshort_ref[i, j : j + 1, :] = scale * (x_tot[3 + k : 4 + k, :] + total(item3(3 + k)))
    gskip_ref[...] = scale * x_tot[9:10, :]

    rank_h = lax.broadcasted_iota(jnp.int32, (RUNS, half), 0).astype(F32)
    for h in range(2):
        lanes = slice(h * half, (h + 1) * half)
        a, p = [], []
        for m in range(MODES):
            lam = lams[m, :, lanes]
            back = jnp.exp(lam * (float(run) * (rank_h - float(RUNS - 1))))
            a.append(jnp.exp(-lam))
            p.append(coefs[m, :, lanes] * (sloc[m, :, lanes] + back * s_dev[m : m + 1, lanes]))
        for r in range(run - 1, -1, -1):
            at = slice(RUNS * r, RUNS * (r + 1))
            p = [x * d for x, d in zip(p, a)]
            terms = p
            while len(terms) > 1:
                terms = [u + w for u, w in zip(terms[::2], terms[1::2])]
            longs[at, lanes] += terms[0]

    gated = longs[...] + skip * gf[...]
    gs[0, :rows, :] = gq[...]
    gs[1, :rows, :] = gated * feat[1]
    gs[2, :rows, :] = gated * feat[0]
    ahead_long = [
        total(coef_t * s_dev),
        total(coef_t * (s_dev - ahead_gf[0]) * jnp.exp(lam_t)),
    ]
    last = lax.broadcasted_iota(jnp.int32, (RUNS, width), 0) == RUNS - 1
    for k in range(2):
        ahead_gated = (ahead_long[k] + skip * ahead_gf[k]) * has_after
        beyond = (ahead_gq[k], ahead_gated * ahead_f[2][k], ahead_gated * ahead_f[1][k])
        for i in range(3):
            head = pltpu.roll(gs[i, RUNS * k : RUNS * (k + 1), :], RUNS - 1, axis=0)
            gs[i, rows + RUNS * k : rows + RUNS * (k + 1), :] = jnp.where(last, beyond[i], head)
    gather = jnp.where(col == RUNS * (row % run) + row // run, 1.0, 0.0).astype(BF16)
    for i in range(3):
        made = (
            tap(i, 0) * gs[i, :rows, :]
            + tap(i, 1) * gs[i, RUNS : rows + RUNS, :]
            + tap(i, 2) * gs[i, 2 * RUNS : rows + 2 * RUNS, :]
        )
        gp_ref[i] = jnp.dot(gather, made.astype(BF16), preferred_element_type=F32).astype(BF16)

    to_next.wait_send()
    to_prev.wait_send()
    others = pl.ds(0, group - 1)
    pltpu.make_async_copy(sbuf.at[others], sbuf.at[others], a_send).wait()
    pltpu.make_async_copy(bb.at[pl.ds(0, n_blocks - 1)], bb.at[pl.ds(0, n_blocks - 1)], b_send).wait()
    pltpu.make_async_copy(cbuf.at[others], cbuf.at[others], c_send).wait()


def solution(mesh):
    n_ctx = mesh.shape["ctx"]
    n_blocks = n_ctx // 32

    def body(projections, filtered, cotangent, short_taps, residues, pole_rates, skip_gain):
        rows, width = filtered.shape
        half = width // 2
        vmem = pl.BlockSpec(memory_space=pltpu.VMEM)
        full = (rows, width)
        out = pl.pallas_call(
            functools.partial(kernel, (n_ctx, n_blocks)),
            out_shape=(
                jax.ShapeDtypeStruct((3,) + full, BF16),
                jax.ShapeDtypeStruct((3, 3, width), F32),
                jax.ShapeDtypeStruct((width, MODES), F32),
                jax.ShapeDtypeStruct((width, MODES), F32),
                jax.ShapeDtypeStruct((1, width), F32),
            ),
            in_specs=[vmem] * 7,
            out_specs=[vmem] * 5,
            scratch_shapes=[
                pltpu.VMEM((3, rows + 16, width), F32),
                pltpu.VMEM((2,) + full, F32),
                pltpu.VMEM(full, F32),
                pltpu.VMEM(full, F32),
                pltpu.VMEM(full, F32),
                pltpu.VMEM((6,) + full, F32),
                pltpu.VMEM(full, F32),
                pltpu.VMEM((MODES, RUNS, width), F32),
                pltpu.VMEM((MODES, RUNS, width), F32),
                pltpu.VMEM((2 * MODES, RUNS, half), F32),
                pltpu.VMEM((2 * MODES, RUNS, half), F32),
                pltpu.VMEM((MODES, RUNS, width), F32),
                pltpu.VMEM((6, RUNS, width), F32),
                pltpu.VMEM((MODES, ROWS, width), F32),
                pltpu.VMEM((32, ROWS, half), BF16),
                pltpu.VMEM((32, ROWS, half), BF16),
                pltpu.VMEM((32 * ROWS, half), F32),
                pltpu.VMEM((4, ROWS, half), BF16),
                pltpu.VMEM((4, n_blocks, ROWS, half), BF16),
                pltpu.VMEM((4 * n_blocks * ROWS, half), F32),
                pltpu.VMEM((4 * n_blocks, half), F32),
                pltpu.VMEM((32, ROWS, half), BF16),
                pltpu.VMEM((32, ROWS, half), BF16),
                pltpu.VMEM((3, rows + 16, width), F32),
                pltpu.VMEM((16, width), F32),
                pltpu.VMEM((8, width), F32),
                pltpu.VMEM((8, width), F32),
                pltpu.VMEM((16, width), F32),
                pltpu.SemaphoreType.DMA((2,)),
                pltpu.SemaphoreType.DMA((2,)),
                pltpu.SemaphoreType.DMA,
                pltpu.SemaphoreType.DMA,
                pltpu.SemaphoreType.DMA,
                pltpu.SemaphoreType.DMA,
                pltpu.SemaphoreType.DMA,
                pltpu.SemaphoreType.DMA,
            ],
            compiler_params=pltpu.CompilerParams(
                collective_id=0, has_side_effects=True, vmem_limit_bytes=40 * 1024 * 1024
            ),
        )(projections, filtered, cotangent, short_taps, residues, pole_rates, skip_gain.reshape(1, width))
        return out[0], out[1], out[2], out[3], out[4].reshape(width)

    return jax.shard_map(
        body,
        mesh=mesh,
        in_specs=(
            P(None, "ctx", "ch"),
            P("ctx", "ch"),
            P("ctx", "ch"),
            P(None, None, "ch"),
            P("ch", None),
            P("ch", None),
            P("ch"),
        ),
        out_specs=(
            P(None, "ctx", "ch"),
            P(None, None, "ch"),
            P("ch", None),
            P("ch", None),
            P("ch"),
        ),
        check_vma=False,
    )
```

time: 798 us -> 50.7 us (0.06); the launches traced: 782 us -> 50.4 us
  blocking collectives: 527 us -> 0 us
  waiting for transfers between devices: 113 us -> 0 us
  other arithmetic: 56.9 us -> 0 us
  Pallas kernels: 0 us -> 43.9 us
  starting transfers between devices: 42 us -> 0 us
  matrix products: 18.3 us -> 0 us
  local copies, waits for them, and re-layouts: 22.1 us -> 5.83 us
    psum x1 -> x0, blocking collectives: 486 us -> none  [body(): lax.psum((residue_owned, rate_owned, skip_term, jnp.stack(tap_terms, axis...]
    all_to_all x3 -> x0, waiting for transfers between devices: 109 us -> none  [the longest x2 55.2 us: seq_transpose(): lax.all_to_all(blocks, 'ctx', split_axis=0, concat_axis=0, tiled=True)]
    pallas_call x0 -> x1, Pallas kernels: none -> 43.9 us  [body(): pl.pallas_call(functools.partial(kernel, (n_ctx, n_blocks)), out_shape=(j...]
    all_to_all x1 -> x0, blocking collectives: 41.5 us -> none  [freq_transpose(): lax.all_to_all(blocks.astype(jnp.bfloat16), 'ctx', split_axis=0, concat_a...]
    all_to_all x3 -> x0, starting transfers between devices: 33.1 us -> none  [the longest x2 25.2 us: seq_transpose(): lax.all_to_all(blocks, 'ctx', split_axis=0, concat_axis=0, tiled=True)]
    dot_general x12 -> x0, matrix products: 18.3 us -> none  [the longest x2 4.25 us: apply_complex(): jnp.einsum(formula, matrix_imag, data_real, precision=highest)]
    mul x39 -> x0, other arithmetic: 15.9 us -> none  [the longest x16 11.7 us: one_mode(): jnp.sum(cross_real * slope_real + cross_imag * slope_imag, axis=(0, 1))]
    reduce_sum x18 -> x0, other arithmetic: 15.5 us -> none  [the longest x16 14.1 us: one_mode(): jnp.sum(cross_real * slope_real + cross_imag * slope_imag, axis=(0, 1))]
  transfers between devices with their start and end apart: 5 -> 0, of which waited for: 5 -> 0; matrix products, arithmetic and copies ran while one was open for 0% -> 0% of each run, Pallas kernels for 0% -> 0%
where the time goes in v1:
time: 50.7 us; the launch traced here: 50.4 us
  Pallas kernels  43.9 us (87%)
  local copies, waits for them, and re-layouts  5.83 us (11%)
  between operations  0.7 us (1%)
    pallas_call x1, Pallas kernels, body(): pl.pallas_call(functools.partial(kernel, (n_ctx, n_blocks)), out_shape=(j...  43.9 us
    unnamed x19, local copies, waits for them, and re-layouts  5.83 us

profile of v1, /device:TPU:1, one launch (start us, length us, event | category | flops | bytes accessed | tf_op | source)
XLA Modules:
  0.0 50.4 jit_solution(7830604784817112194)
XLA Ops:
  0.6 0.0 copy-start.5
  0.6 0.0 copy-start.1
  0.7 0.0 copy-start.2
  0.7 0.9 %copy.12.res_ref = f32[256,16]{1,0:T(8,128)S(1)} copy(f32[256,16]{0,1:T(8,128)} %param.11) | data formatting | bytes 32768 | tf_op args[4]
  1.5 0.0 copy-done.5
  1.5 0.0 copy-start.3
  1.5 0.0 copy-start.4
  1.6 0.1 copy.13.rate_ref
  1.7 0.0 copy-done.1
  1.7 0.0 copy-done.2
  1.7 0.6 %copy-done.3 = f32[3,3,256]{2,1,0:T(4,128)S(1)} copy-done((f32[3,3,256]{2,1,0:T(4,128)S(1)}, f32[3,3,256]{2,1,0:T(4,128)}, u32[]{:S(2)}) %copy-start.3) | copy-done | bytes 9240
  2.3 0.0 copy-done.4
  2.3 0.0 copy-start
  2.3 1.0 %copy-done = bf16[3,256,256]{2,1,0:T(8,128)(2,1)S(1)} copy-done((bf16[3,256,256]{2,1,0:T(8,128)(2,1)S(1)}, bf16[3,256,256]{2,1,0:T(8,128)(2,1)}, u32[]{:S(2)}) %copy-start) | copy-done | bytes 393240
  3.3 43.9 %shard_map.110 = (bf16[3,256,256]{2,1,0:T(8,128)(2,1)S(1)}, f32[3,3,256]{2,1,0:T(4,128)S(1)}, f32[256,16]{1,0:T(8,128)S(1)}, f32[256,16]{1,0:T(8,128)S(1)}, f32[1,256]{1,0:T(1,128)S(1)}) custom-call(bf16[3,256,256]{2,1,0:T(8,128)(2,1)S(1)} %copy-done, bf16[256,256]{1,0:T(8,128)(2,1)S(1)} %copy-done.1, bf16[256,256]{1,0:T(8,128)(2,1)S(1)} %copy-done.2, ...), custom_call_target="tpu_custom_call" | custom-call | tf_op jit(solution)/shard_map/pallas_call | solution.py:451
  47.2 0.7 %copy.14 = f32[256,16]{0,1:T(8,128)} copy(f32[256,16]{1,0:T(8,128)S(1)} %get-tuple-element.17) | data formatting | bytes 32768
  47.9 0.7 %copy.15 = f32[256,16]{0,1:T(8,128)} copy(f32[256,16]{1,0:T(8,128)S(1)} %get-tuple-element.18) | data formatting | bytes 32768
  48.5 0.7 %copy.19 = bf16[3,256,256]{2,1,0:T(8,128)(2,1)} copy(bf16[3,256,256]{2,1,0:T(8,128)(2,1)S(1)} %get-tuple-element.25) | data formatting | bytes 786432
  49.3 0.6 %copy.20 = f32[3,3,256]{2,1,0:T(4,128)} copy(f32[3,3,256]{2,1,0:T(4,128)S(1)} %get-tuple-element.26) | data formatting | bytes 18432
  49.9 0.6 %copy.21 = f32[256]{0:T(256)} copy(f32[256]{0:T(256)S(1)} %bitcast.2) | data formatting | bytes 2048
Async XLA Ops:
  0.6 0.9 %copy-start.5 = (f32[256,16]{0,1:T(8,128)S(1)}, f32[256,16]{0,1:T(8,128)}, u32[]{:S(2)}) copy-start(f32[256,16]{0,1:T(8,128)} %param.12) | copy-start | bytes 49156
  0.6 1.0 %copy-start.1 = (bf16[256,256]{1,0:T(8,128)(2,1)S(1)}, bf16[256,256]{1,0:T(8,128)(2,1)}, u32[]{:S(2)}) copy-start(bf16[256,256]{1,0:T(8,128)(2,1)} %filt_ref.1) | copy-start | bytes 393220
  0.7 1.0 %copy-start.2 = (bf16[256,256]{1,0:T(8,128)(2,1)S(1)}, bf16[256,256]{1,0:T(8,128)(2,1)}, u32[]{:S(2)}) copy-start(bf16[256,256]{1,0:T(8,128)(2,1)} %cot_ref.1) | copy-start | bytes 393220
  1.5 0.7 %copy-start.3 = (f32[3,3,256]{2,1,0:T(4,128)S(1)}, f32[3,3,256]{2,1,0:T(4,128)}, u32[]{:S(2)}) copy-start(f32[3,3,256]{2,1,0:T(4,128)} %taps_ref.1) | copy-start | bytes 27652
  1.5 0.7 %copy-start.4 = (f32[256]{0:T(256)S(1)}, f32[256]{0:T(256)}, u32[]{:S(2)}) copy-start(f32[256]{0:T(256)} %param.13) | copy-start | bytes 3076
  2.3 1.0 %copy-start = (bf16[3,256,256]{2,1,0:T(8,128)(2,1)S(1)}, bf16[3,256,256]{2,1,0:T(8,128)(2,1)}, u32[]{:S(2)}) copy-start(bf16[3,256,256]{2,1,0:T(8,128)(2,1)} %proj_ref.1) | copy-start | bytes 1179652

commit v2 on v1

--- a/solution.py
+++ b/solution.py
@@ -51,6 +51,18 @@
 
 def kernel(
     geometry,
+    proj_hbm,
+    filt_hbm,
+    cot_hbm,
+    taps_hbm,
+    res_hbm,
+    rate_hbm,
+    skip_hbm,
+    gp_ref,
+    gshort_ref,
+    gres_ref,
+    grate_ref,
+    gskip_ref,
     proj_ref,
     filt_ref,
     cot_ref,
@@ -58,11 +70,6 @@
     res_ref,
     rate_ref,
     skip_ref,
-    gp_ref,
-    gshort_ref,
-    gres_ref,
-    grate_ref,
-    gskip_ref,
     ext,
     feat,
     gf,
@@ -87,10 +94,9 @@
     cbuf,
     cr,
     gs,
-    halo_out_prev,
-    halo_out_next,
     halo_prev,
     halo_next,
+    in_sem,
     halo_send,
     halo_recv,
     a_send,
@@ -129,16 +135,27 @@
     for d in (before, after):
         pl.semaphore_signal(barrier, inc=1, device_id={"ctx": d}, device_id_type=MESH)
 
-    for i in range(3):
-        halo_out_next[2 * i : 2 * i + 2, :] = proj_ref[i, rows - 16 :, :].astype(F32)[14:16]
-        halo_out_prev[2 * i : 2 * i + 2, :] = proj_ref[i, :16, :].astype(F32)[0:2]
-    halo_out_next[6:8, :] = jnp.zeros((2, width), F32)
-    halo_out_prev[6:8, :] = cot_ref[:16, :].astype(F32)[0:2]
-    halo_out_prev[8:10, :] = filt_ref[:16, :].astype(F32)[0:2]
-    halo_out_prev[10:16, :] = jnp.zeros((6, width), F32)
-
-    lam_t = jnp.transpose(rate_ref[...]) * (1.0 / tokens)
-    coef_t = jnp.transpose(res_ref[...]) * jnp.sqrt(lam_t)
+    held = (
+        (taps_hbm, taps_ref),
+        (res_hbm, res_ref),
+        (rate_hbm, rate_ref),
+        (skip_hbm, skip_ref),
+        (proj_hbm, proj_ref),
+        (cot_hbm, cot_ref),
+        (filt_hbm, filt_ref),
+    )
+    loads = [pltpu.make_async_copy(src, dst, in_sem.at[i]) for i, (src, dst) in enumerate(held)]
+    for load in loads:
+        load.start()
+
+    row = lax.broadcasted_iota(jnp.int32, (rows, rows), 0)
+    col = lax.broadcasted_iota(jnp.int32, (rows, rows), 1)
+    spread = jnp.where(col == run * (row % RUNS) + row // RUNS, 1.0, 0.0).astype(BF16)
+    for load in loads[:4]:
+        load.wait()
+
+    lam_t = rate_ref[...] * (1.0 / tokens)
+    coef_t = res_ref[...] * jnp.sqrt(lam_t)
     for m in range(MODES):
         lam_m = jnp.broadcast_to(lam_t[m : m + 1, :], (RUNS, width))
         coef_m = jnp.broadcast_to(coef_t[m : m + 1, :], (RUNS, width))
@@ -148,53 +165,57 @@
             owner_lam[2 * m + h] = lam_m[:, h * half : (h + 1) * half]
             owner_coef[2 * m + h] = coef_m[:, h * half : (h + 1) * half]
 
-    row = lax.broadcasted_iota(jnp.int32, (rows, rows), 0)
-    col = lax.broadcasted_iota(jnp.int32, (rows, rows), 1)
-    spread = jnp.where(col == run * (row % RUNS) + row // RUNS, 1.0, 0.0).astype(BF16)
-
     def placed(x):
         return jnp.dot(spread, x, preferred_element_type=F32)
 
+    first = lax.broadcasted_iota(jnp.int32, (RUNS, width), 0) == 0
+    first_two = lax.broadcasted_iota(jnp.int32, (2 * RUNS, width), 0) % RUNS == 0
+    for load in loads[4:]:
+        load.wait()
     for i in range(3):
         ext[i, 16:, :] = placed(proj_ref[i])
+        for back in (2, 1):
+            tail = pltpu.roll(ext[i, 16 + RUNS * (run - back) : 16 + RUNS * (run - back + 1), :], 1, axis=0)
+            ext[i, 16 - 8 * back : 24 - 8 * back, :] = jnp.where(first, 0.0, tail)
+
+    def tap(i, j):
+        return taps_ref[i, j : j + 1, :]
+
+    def shifted(i, j):
+        return ext[i, 16 - 8 * j : 16 - 8 * j + rows, :]
+
+    def masked(x):
+        return jnp.concatenate([jnp.where(first_two, 0.0, x[: 2 * RUNS]), x[2 * RUNS :]], axis=0)
+
     cot = placed(cot_ref[...])
     gq[...] = cot * placed(filt_ref[...])
-
-    pl.semaphore_wait(barrier, group - 1 + n_blocks - 1 + 2)
-    to_next = pltpu.make_async_remote_copy(
-        halo_out_next, halo_prev, halo_send.at[0], halo_recv.at[0], device_id={"ctx": after}, device_id_type=MESH
-    )
-    to_prev = pltpu.make_async_remote_copy(
-        halo_out_prev, halo_next, halo_send.at[1], halo_recv.at[1], device_id={"ctx": before}, device_id_type=MESH
-    )
-    to_next.start()
-    to_prev.start()
-    to_next.wait_recv()
-
-    first = lax.broadcasted_iota(jnp.int32, (RUNS, width), 0) == 0
-    has_before = jnp.where(me > 0, 1.0, 0.0)
-    for i in range(3):
-        for back in (2, 1):
-            tail = pltpu.roll(ext[i, 16 + RUNS * (run - back) : 16 + RUNS * (run - back + 1), :], 1, axis=0)
-            rim = halo_prev[2 * i + 2 - back : 2 * i + 3 - back, :] * has_before
-            ext[i, 16 - 8 * back : 24 - 8 * back, :] = jnp.where(first, rim, tail)
-
-    def tap(i, j):
-        return taps_ref[i, j : j + 1, :]
-
-    def shifted(i, j):
-        return ext[i, 16 - 8 * j : 16 - 8 * j + rows, :]
-
     for i in range(3):
         made = tap(i, 0) * shifted(i, 0) + tap(i, 1) * shifted(i, 1) + tap(i, 2) * shifted(i, 2)
         if i == 0:
-            gf[...] = cot * made
+            gf[...] = masked(cot * made)
         else:
             feat[i - 1] = made
-    gv[...] = feat[0] * feat[1]
+    gv[...] = masked(feat[0] * feat[1])
     for j in range(3):
-        ys[j] = feat[1] * shifted(1, j)
-        ys[3 + j] = feat[0] * shifted(2, j)
+        ys[j] = masked(feat[1] * shifted(1, j))
+        ys[3 + j] = masked(feat[0] * shifted(2, j))
+
+    pl.semaphore_wait(barrier, group - 1 + n_blocks - 1 + 2)
+    last_rows, first_rows = pl.ds(rows - 16, 16), pl.ds(0, 16)
+    rims = (
+        (proj_ref.at[:, last_rows], halo_prev, after),
+        (proj_ref.at[:, first_rows], halo_next.at[pl.ds(0, 3)], before),
+        (cot_ref.at[first_rows], halo_next.at[3], before),
+        (filt_ref.at[first_rows], halo_next.at[4], before),
+    )
+    rims = [
+        pltpu.make_async_remote_copy(
+            src, dst, halo_send.at[i], halo_recv.at[i], device_id={"ctx": to}, device_id_type=MESH
+        )
+        for i, (src, dst, to) in enumerate(rims)
+    ]
+    for rim in rims:
+        rim.start()
     longs[...] = jnp.zeros_like(longs)
     crosses[...] = jnp.zeros_like(crosses)
 
@@ -223,33 +244,91 @@
         inner, inner_slope, s_loc, sp_loc = suffix(state, slope, lam, run, RUNS)
         sloc[m] = s_loc
         weight = jnp.exp(lam * (float(run) * (rank - float(RUNS - 1))))
-        sums[m, ROW_L : ROW_L + 1, :] = inner[0:1, :]
-        sums[m, ROW_LP : ROW_LP + 1, :] = inner_slope[0:1, :]
-        sums[m, ROW_V : ROW_V + 1, :] = total(weight * v)
-        sums[m, ROW_VP : ROW_VP + 1, :] = total(weight * (vp + float(run) * (float(RUNS - 1) - rank) * v))
+        at = m * ROWS
+
+        def put(k, value):
+            for h in range(2):
+                sums[pl.ds(h * MODES * ROWS + at + k, 1), :] = value[:, h * half : (h + 1) * half]
+
+        put(ROW_L, inner[0:1, :])
+        put(ROW_LP, inner_slope[0:1, :])
+        put(ROW_V, total(weight * v))
+        put(ROW_VP, total(weight * (vp + float(run) * (float(RUNS - 1) - rank) * v)))
         state_in = coef * s_loc
         for k in range(6):
-            sums[m, ROW_W + k : ROW_W + k + 1, :] = total(weight * w[k])
+            put(ROW_W + k, total(weight * w[k]))
             crosses[k] += state_in * w[k]
-        pair = (total(r_sum + v * s_loc), total(d_sum + vp * s_loc + v * sp_loc))
-        for at, value in zip((ROW_R, ROW_D, ROW_X), pair + (jnp.zeros((1, width), F32),)):
-            sums[m, at : at + 1, :] = value
-            sums[m, at + REST : at + REST + 1, :] = rest(value)
+        put(ROW_R, total(r_sum + v * s_loc))
+        put(ROW_D, total(d_sum + vp * s_loc + v * sp_loc))
         return 0
 
     lax.fori_loop(0, MODES, one_mode, 0)
 
     skip = skip_ref[...]
     inner_gated = longs[...] + skip * gf[...]
-    plain = [total(gq[...] * shifted(0, j)) for j in range(3)]
+    own_query = masked(gq[...])
+    plain = [total(own_query * shifted(0, j)) for j in range(3)]
     plain += [total(inner_gated * ys[k]) + total(crosses[k]) for k in range(6)]
     plain.append(total(gf[...] * gv[...]))
-    for m, value in enumerate(plain):
-        sums[m, ROW_X : ROW_X + 1, :] = value
-        sums[m, ROW_X + REST : ROW_X + REST + 1, :] = rest(value)
+
+    rims[0].wait_recv()
+    has_before = jnp.where(me > 0, 1.0, 0.0)
+    before_rows = [halo_prev[i].astype(F32)[14:16] * has_before for i in range(3)]
+    x = [
+        {-2: before_rows[i][0:1], -1: before_rows[i][1:2], 0: ext[i, 16:17, :], 1: ext[i, 24:25, :]}
+        for i in range(3)
+    ]
+    f = [[tap(i, 0) * x[i][t] + tap(i, 1) * x[i][t - 1] + tap(i, 2) * x[i][t - 2] for t in range(2)] for i in range(3)]
+    cot_two = [cot[0:1], cot[RUNS : RUNS + 1]]
+    gf_two = [cot_two[t] * f[0][t] for t in range(2)]
+    gv_two = [f[1][t] * f[2][t] for t in range(2)]
+    ys_two = [[f[2][t] * x[1][t - j] for j in range(3)] + [f[1][t] * x[2][t - j] for j in range(3)] for t in range(2)]
+
+    def each_mode(k):
+        return jnp.concatenate(
+            [sums[pl.ds(h * MODES * ROWS + k, MODES, stride=ROWS), :] for h in range(2)], axis=1
+        )
+
+    def keep(k, value):
+        for h in range(2):
+            sums[pl.ds(h * MODES * ROWS + k, MODES, stride=ROWS), :] = value[:, h * half : (h + 1) * half]
+
+    a_t = jnp.exp(-lam_t)
+    back_two = jnp.exp(2.0 * lam_t)
+    two, two_slope = each_mode(ROW_L), each_mode(ROW_LP)
+    two, two_slope = back_two * two, back_two * (two_slope - 2.0 * two)
+    slope_1 = a_t * (two_slope + two)
+    state_1 = gf_two[1] + a_t * two
+    slope_0 = a_t * (slope_1 + state_1)
+    state_0 = gf_two[0] + a_t * state_1
+    decays = [jnp.exp(lam_t * -float(rows)), jnp.exp(lam_t * -float(rows - 1))]
+    parts = [decays[t] * gv_two[t] for t in range(2)]
+    keep(ROW_L, state_0)
+    keep(ROW_LP, slope_0)
+    keep(ROW_V, each_mode(ROW_V) + parts[0] + parts[1])
+    keep(ROW_VP, each_mode(ROW_VP) + float(rows) * parts[0] + float(rows - 1) * parts[1])
+    for k in range(6):
+        keep(ROW_W + k, each_mode(ROW_W + k) + decays[0] * ys_two[0][k] + decays[1] * ys_two[1][k])
+    r_all = each_mode(ROW_R) + gv_two[1] * state_1 + gv_two[0] * state_0
+    d_all = each_mode(ROW_D) + gv_two[1] * slope_1 + gv_two[0] * slope_0
+    keep(ROW_R, r_all)
+    keep(ROW_R + REST, rest(r_all))
+    keep(ROW_D, d_all)
+    keep(ROW_D + REST, rest(d_all))
+    gated_two = [total(coef_t * state_0) + skip * gf_two[0], total(coef_t * state_1) + skip * gf_two[1]]
+    for t in range(2):
+        for j in range(3):
+            plain[j] = plain[j] + gq[RUNS * t : RUNS * t + 1, :] * x[0][t - j]
+        for k in range(6):
+            plain[3 + k] = plain[3 + k] + gated_two[t] * ys_two[t][k]
+        plain[9] = plain[9] + gf_two[t] * gv_two[t]
+    plain = jnp.concatenate(plain + [jnp.zeros((MODES - len(plain), width), F32)], axis=0)
+    keep(ROW_X, plain)
+    keep(ROW_X + REST, rest(plain))
     for m in range(MODES):
         for h in range(2):
-            sbuf[2 * m + h] = sums[m, :, h * half : (h + 1) * half].astype(BF16)
+            at = (h * MODES + m) * ROWS
+            sbuf[2 * m + h] = sums[at : at + ROWS, :].astype(BF16)
 
     own_a = pltpu.make_async_copy(sbuf.at[pos], rbuf.at[pos], a_recv)
     own_a.start()
@@ -258,6 +337,15 @@
         pltpu.make_async_remote_copy(
             sbuf.at[p], rbuf.at[pos], a_send, a_recv, device_id={"ctx": member(p)}, device_id_type=MESH
         ).start()
+
+    direct = [total(coef_t) * gf_two[0] + total(coef_t * a_t) * gf_two[1], total(coef_t) * gf_two[1]]
+    for t in range(2):
+        at = slice(RUNS * t, RUNS * t + 1)
+        gf[at, :] = gf_two[t]
+        longs[at, :] += direct[t]
+        for i in (1, 2):
+            feat[i - 1, at, :] = f[i][t]
+
     pltpu.make_async_copy(rbuf, rbuf, a_recv).wait()
 
     lam_o = owner_lam[pos]
@@ -353,19 +441,20 @@
             cbuf.at[p], cr.at[pos], c_send, c_recv, device_id={"ctx": member(p)}, device_id_type=MESH
         ).start()
 
-    to_prev.wait_recv()
+    for rim in rims[1:]:
+        rim.wait_recv()
     has_after = jnp.where(me < n_ctx - 1, 1.0, 0.0)
-    ahead = halo_next[...] * has_after
+    ahead = [halo_next[i].astype(F32) * has_after for i in range(5)]
 
     def ahead_feat(i, k):
         mine = [ext[i, 16 + RUNS * (run - 1 - b) + RUNS - 1 : 16 + RUNS * (run - b), :] for b in range(2)]
         if k == 0:
-            return tap(i, 0) * ahead[2 * i : 2 * i + 1] + tap(i, 1) * mine[0] + tap(i, 2) * mine[1]
-        return tap(i, 0) * ahead[2 * i + 1 : 2 * i + 2] + tap(i, 1) * ahead[2 * i : 2 * i + 1] + tap(i, 2) * mine[0]
+            return tap(i, 0) * ahead[i][0:1] + tap(i, 1) * mine[0] + tap(i, 2) * mine[1]
+        return tap(i, 0) * ahead[i][1:2] + tap(i, 1) * ahead[i][0:1] + tap(i, 2) * mine[0]
 
     ahead_f = [[ahead_feat(i, k) for k in range(2)] for i in range(3)]
-    ahead_gf = [ahead[6 + k : 7 + k] * ahead_f[0][k] for k in range(2)]
-    ahead_gq = [ahead[6 + k : 7 + k] * ahead[8 + k : 9 + k] for k in range(2)]
+    ahead_gf = [ahead[3][k : k + 1] * ahead_f[0][k] for k in range(2)]
+    ahead_gq = [ahead[3][k : k + 1] * ahead[4][k : k + 1] for k in range(2)]
 
     pltpu.make_async_copy(cr, cr, c_recv).wait()
     flat[...] = cr[...].astype(F32).reshape(group * ROWS, half)
@@ -379,10 +468,8 @@
     s_dev = item3(0) + item3(13)
     r_tot, d_tot, x_tot = item3(1) + item3(10), item3(2) + item3(11), item3(9) + item3(12)
     root = jnp.sqrt(lam_t)
-    res_t = jnp.transpose(res_ref[...])
-    rate_t = jnp.transpose(rate_ref[...])
-    gres_ref[...] = jnp.transpose(scale * root * r_tot)
-    grate_ref[...] = jnp.transpose(scale * res_t * root * (0.5 / rate_t * r_tot - d_tot * (1.0 / tokens)))
+    gres_ref[...] = scale * root * r_tot
+    grate_ref[...] = scale * res_ref[...] * root * (0.5 / rate_ref[...] * r_tot - d_tot * (1.0 / tokens))
     for j in range(3):
         gshort_ref[0, j : j + 1, :] = scale * x_tot[j : j + 1, :]
         for i in (1, 2):
@@ -431,12 +518,25 @@
         )
         gp_ref[i] = jnp.dot(gather, made.astype(BF16), preferred_element_type=F32).astype(BF16)
 
-    to_next.wait_send()
-    to_prev.wait_send()
+    for rim in rims:
+        rim.wait_send()
     others = pl.ds(0, group - 1)
     pltpu.make_async_copy(sbuf.at[others], sbuf.at[others], a_send).wait()
     pltpu.make_async_copy(bb.at[pl.ds(0, n_blocks - 1)], bb.at[pl.ds(0, n_blocks - 1)], b_send).wait()
     pltpu.make_async_copy(cbuf.at[others], cbuf.at[others], c_send).wait()
+
+
+def hand_over(*refs):
+    count = (len(refs) - 1) // 2
+    sems = refs[-1]
+    copies = [
+        pltpu.make_async_copy(src, dst, sems.at[i])
+        for i, (src, dst) in enumerate(zip(refs[:count], refs[count : 2 * count]))
+    ]
+    for copy in copies:
+        copy.start()
+    for copy in copies:
+        copy.wait()
 
 
 def solution(mesh):
@@ -448,18 +548,21 @@
         half = width // 2
         vmem = pl.BlockSpec(memory_space=pltpu.VMEM)
         full = (rows, width)
+        made = (
+            jax.ShapeDtypeStruct((3,) + full, BF16),
+            jax.ShapeDtypeStruct((3, 3, width), F32),
+            jax.ShapeDtypeStruct((MODES, width), F32),
+            jax.ShapeDtypeStruct((MODES, width), F32),
+            jax.ShapeDtypeStruct((1, width), F32),
+        )
+        args = (projections, filtered, cotangent, short_taps, residues.T, pole_rates.T, skip_gain.reshape(1, width))
         out = pl.pallas_call(
             functools.partial(kernel, (n_ctx, n_blocks)),
-            out_shape=(
-                jax.ShapeDtypeStruct((3,) + full, BF16),
-                jax.ShapeDtypeStruct((3, 3, width), F32),
-                jax.ShapeDtypeStruct((width, MODES), F32),
-                jax.ShapeDtypeStruct((width, MODES), F32),
-                jax.ShapeDtypeStruct((1, width), F32),
-            ),
-            in_specs=[vmem] * 7,
+            out_shape=[pltpu.VMEM(x.shape, x.dtype) for x in made],
+            in_specs=[pl.BlockSpec(memory_space=pltpu.HBM)] * 7,
             out_specs=[vmem] * 5,
-            scratch_shapes=[
+            scratch_shapes=[pltpu.VMEM(x.shape, x.dtype) for x in args]
+            + [
                 pltpu.VMEM((3, rows + 16, width), F32),
                 pltpu.VMEM((2,) + full, F32),
                 pltpu.VMEM(full, F32),
@@ -473,7 +576,7 @@
                 pltpu.VMEM((2 * MODES, RUNS, half), F32),
                 pltpu.VMEM((MODES, RUNS, width), F32),
                 pltpu.VMEM((6, RUNS, width), F32),
-                pltpu.VMEM((MODES, ROWS, width), F32),
+                pltpu.VMEM((2 * MODES * ROWS, half), F32),
                 pltpu.VMEM((32, ROWS, half), BF16),
                 pltpu.VMEM((32, ROWS, half), BF16),
                 pltpu.VMEM((32 * ROWS, half), F32),
@@ -484,12 +587,11 @@
                 pltpu.VMEM((32, ROWS, half), BF16),
                 pltpu.VMEM((32, ROWS, half), BF16),
                 pltpu.VMEM((3, rows + 16, width), F32),
-                pltpu.VMEM((16, width), F32),
-                pltpu.VMEM((8, width), F32),
-                pltpu.VMEM((8, width), F32),
-                pltpu.VMEM((16, width), F32),
-                pltpu.SemaphoreType.DMA((2,)),
-                pltpu.SemaphoreType.DMA((2,)),
+                pltpu.VMEM((3, 16, width), BF16),
+                pltpu.VMEM((5, 16, width), BF16),
+                pltpu.SemaphoreType.DMA((7,)),
+                pltpu.SemaphoreType.DMA((4,)),
+                pltpu.SemaphoreType.DMA((4,)),
                 pltpu.SemaphoreType.DMA,
                 pltpu.SemaphoreType.DMA,
                 pltpu.SemaphoreType.DMA,
@@ -500,8 +602,15 @@
             compiler_params=pltpu.CompilerParams(
                 collective_id=0, has_side_effects=True, vmem_limit_bytes=40 * 1024 * 1024
             ),
-        )(projections, filtered, cotangent, short_taps, residues, pole_rates, skip_gain.reshape(1, width))
-        return out[0], out[1], out[2], out[3], out[4].reshape(width)
+        )(*(pltpu.with_memory_space_constraint(x, pltpu.HBM) for x in args))
+        out = pl.pallas_call(
+            hand_over,
+            out_shape=[pltpu.HBM(x.shape, x.dtype) for x in made],
+            in_specs=[vmem] * 5,
+            out_specs=[pl.BlockSpec(memory_space=pltpu.HBM)] * 5,
+            scratch_shapes=[pltpu.SemaphoreType.DMA((5,))],
+        )(*(pltpu.with_memory_space_constraint(x, pltpu.VMEM) for x in out))
+        return out[0], out[1], out[2].T, out[3].T, out[4].reshape(width)
 
     return jax.shard_map(
         body,

time: 50.7 us -> 42.2 us (0.83)
  local copies, waits for them, and re-layouts: 5.83 us -> 0 us
  Pallas kernels: 43.9 us -> 41.4 us
    unnamed x19 -> x0, local copies, waits for them, and re-layouts: 5.83 us -> none
    pallas_call x1 -> x2, Pallas kernels: 43.9 us -> 41.4 us  [the longest x1 40.6 us: body(): pl.pallas_call(functools.partial(kernel, (n_ctx, n_blocks)), out_shape=[p...]
where the time goes in v2:
time: 42.2 us; the launch traced here: 42.1 us
  Pallas kernels  41.4 us (98%)
  between operations  0.64 us (2%)
    pallas_call x1, Pallas kernels, body(): pl.pallas_call(functools.partial(kernel, (n_ctx, n_blocks)), out_shape=[p...  40.6 us

profile of v2, /device:TPU:1, one launch (start us, length us, event | category | flops | bytes accessed | tf_op | source)
XLA Modules:
  0.0 42.1 jit_solution(10599796024689052098)
XLA Ops:
  0.6 40.6 %shard_map.110 = (bf16[3,256,256]{2,1,0:T(8,128)(2,1)S(1)}, f32[3,3,256]{2,1,0:T(4,128)S(1)}, f32[16,256]{1,0:T(8,128)S(1)}, f32[16,256]{1,0:T(8,128)S(1)}, f32[1,256]{1,0:T(1,128)S(1)}) custom-call(bf16[3,256,256]{2,1,0:T(8,128)(2,1)} %proj_hbm.1, bf16[256,256]{1,0:T(8,128)(2,1)} %filt_hbm.1, bf16[256,256]{1,0:T(8,128)(2,1)} %cot_hbm.1, ...), custom_call_target="tpu_custom_call" | custom-call | tf_op jit(solution)/shard_map/pallas_call | solution.py:559
  41.3 0.8 %shard_map.111 = (bf16[3,256,256]{2,1,0:T(8,128)(2,1)}, f32[3,3,256]{2,1,0:T(4,128)}, f32[16,256]{1,0:T(8,128)}, f32[16,256]{1,0:T(8,128)}, f32[1,256]{1,0:T(1,128)}) custom-call(bf16[3,256,256]{2,1,0:T(8,128)(2,1)S(1)} %get-tuple-element.15.refs_0_, f32[3,3,256]{2,1,0:T(4,128)S(1)} %get-tuple-element.16.refs_1_, f32[16,256]{1,0:T(8,128)S(1)} %get-tuple-element.17.refs_2_, ...), custom_call_target="tpu_custom_call" | custom-call | tf_op jit(solution)/shard_map/pallas_call | solution.py:606

commit v3 on v2

--- a/solution.py
+++ b/solution.py
@@ -74,6 +74,7 @@
     feat,
     gf,
     gv,
+    gz,
     gq,
     ys,
     longs,
@@ -115,26 +116,10 @@
     per_block = 8
     group = 32
     me = lax.axis_index("ctx")
-    y = me // (per_block * n_blocks)
-    zh = (me // per_block) % n_blocks
-    lo = me % per_block
+    y = lax.div(me, per_block * n_blocks)
+    zh = lax.rem(lax.div(me, per_block), n_blocks)
+    lo = lax.rem(me, per_block)
     pos = y * per_block + lo
-
-    def member(p):
-        return (p // per_block) * (per_block * n_blocks) + zh * per_block + p % per_block
-
-    def cousin(b):
-        return y * (per_block * n_blocks) + b * per_block + lo
-
-    before, after = (me + n_ctx - 1) % n_ctx, (me + 1) % n_ctx
-    barrier = pltpu.get_barrier_semaphore()
-    for j in range(1, group):
-        pl.semaphore_signal(barrier, inc=1, device_id={"ctx": member((pos + j) % group)}, device_id_type=MESH)
-    for j in range(1, n_blocks):
-        pl.semaphore_signal(barrier, inc=1, device_id={"ctx": cousin((zh + j) % n_blocks)}, device_id_type=MESH)
-    for d in (before, after):
-        pl.semaphore_signal(barrier, inc=1, device_id={"ctx": d}, device_id_type=MESH)
-
     held = (
         (taps_hbm, taps_ref),
         (res_hbm, res_ref),
@@ -148,6 +133,21 @@
     for load in loads:
         load.start()
 
+    ys_of = [lax.rem(y + d, 4) for d in range(4)]
+    los_of = [lo] + [lax.rem(lo + d, per_block) for d in range(1, per_block)]
+    bases = [v * (per_block * n_blocks) + zh * per_block for v in ys_of]
+    peers = [
+        (ys_of[d] * per_block + los_of[k], bases[d] + los_of[k])
+        for d in (2, 1, 3, 0)
+        for k in (2, 6, 3, 5, 4, 7, 1, 0)
+        if (d, k) != (0, 0)
+    ]
+    cousins = [y * (per_block * n_blocks) + lax.rem(zh + j, n_blocks) * per_block + lo for j in (2, 1, 3)]
+    before, after = lax.rem(me + n_ctx - 1, n_ctx), lax.rem(me + 1, n_ctx)
+    barrier = pltpu.get_barrier_semaphore()
+    for d in cousins + [index for _, index in peers] + [before, after]:
+        pl.semaphore_signal(barrier, inc=1, device_id={"ctx": d}, device_id_type=MESH)
+
     row = lax.broadcasted_iota(jnp.int32, (rows, rows), 0)
     col = lax.broadcasted_iota(jnp.int32, (rows, rows), 1)
     spread = jnp.where(col == run * (row % RUNS) + row // RUNS, 1.0, 0.0).astype(BF16)
@@ -196,6 +196,9 @@
         else:
             feat[i - 1] = made
     gv[...] = masked(feat[0] * feat[1])
+    step_of = lax.broadcasted_iota(jnp.int32, (rows, width), 0) // RUNS
+    to_end = (run - step_of).astype(F32)
+    gz[...] = to_end * gv[...]
     for j in range(3):
         ys[j] = masked(feat[1] * shifted(1, j))
         ys[3 + j] = masked(feat[0] * shifted(2, j))
@@ -226,7 +229,7 @@
         coef = coefs[m]
         a = jnp.exp(-lam)
         zero = jnp.zeros((RUNS, width), F32)
-        state, slope, r_sum, d_sum, v, vp = zero, zero, zero, zero, zero, zero
+        state, slope, r_sum, d_sum, vp = zero, zero, zero, zero, zero
         w = [zero] * 6
         for step in range(run):
             low = slice(RUNS * (run - 1 - step), RUNS * (run - step))
@@ -237,18 +240,16 @@
             gv_low = gv[low, :]
             r_sum = r_sum + gv_low * state
             d_sum = d_sum + gv_low * slope
-            v = a * (v + gv[high, :])
-            vp = a * vp + v
+            vp = a * (vp + gz[high, :])
             for k in range(6):
                 w[k] = a * (w[k] + ys[k, high, :])
+        v = tap(1, 0) * w[0] + tap(1, 1) * w[1] + tap(1, 2) * w[2]
         inner, inner_slope, s_loc, sp_loc = suffix(state, slope, lam, run, RUNS)
         sloc[m] = s_loc
         weight = jnp.exp(lam * (float(run) * (rank - float(RUNS - 1))))
-        at = m * ROWS
-
         def put(k, value):
             for h in range(2):
-                sums[pl.ds(h * MODES * ROWS + at + k, 1), :] = value[:, h * half : (h + 1) * half]
+                sums[pl.ds((h * ROWS + k) * MODES + m, 1), :] = value[:, h * half : (h + 1) * half]
 
         put(ROW_L, inner[0:1, :])
         put(ROW_LP, inner_slope[0:1, :])
@@ -286,12 +287,12 @@
 
     def each_mode(k):
         return jnp.concatenate(
-            [sums[pl.ds(h * MODES * ROWS + k, MODES, stride=ROWS), :] for h in range(2)], axis=1
+            [sums[(h * ROWS + k) * MODES : (h * ROWS + k + 1) * MODES, :] for h in range(2)], axis=1
         )
 
     def keep(k, value):
         for h in range(2):
-            sums[pl.ds(h * MODES * ROWS + k, MODES, stride=ROWS), :] = value[:, h * half : (h + 1) * half]
+            sums[(h * ROWS + k) * MODES : (h * ROWS + k + 1) * MODES, :] = value[:, h * half : (h + 1) * half]
 
     a_t = jnp.exp(-lam_t)
     back_two = jnp.exp(2.0 * lam_t)
@@ -327,15 +328,13 @@
     keep(ROW_X + REST, rest(plain))
     for m in range(MODES):
         for h in range(2):
-            at = (h * MODES + m) * ROWS
-            sbuf[2 * m + h] = sums[at : at + ROWS, :].astype(BF16)
+            sbuf[2 * m + h] = sums[pl.ds(h * ROWS * MODES + m, ROWS, stride=MODES), :].astype(BF16)
 
     own_a = pltpu.make_async_copy(sbuf.at[pos], rbuf.at[pos], a_recv)
     own_a.start()
-    for j in range(1, group):
-        p = (pos + j) % group
+    for p, index in peers:
         pltpu.make_async_remote_copy(
-            sbuf.at[p], rbuf.at[pos], a_send, a_recv, device_id={"ctx": member(p)}, device_id_type=MESH
+            sbuf.at[p], rbuf.at[pos], a_send, a_recv, device_id={"ctx": index}, device_id_type=MESH
         ).start()
 
     direct = [total(coef_t) * gf_two[0] + total(coef_t * a_t) * gf_two[1], total(coef_t) * gf_two[1]]
@@ -393,9 +392,9 @@
 
     own_b = pltpu.make_async_copy(bbuf, bb.at[:, zh], b_recv)
     own_b.start()
-    for j in range(1, n_blocks):
+    for index in cousins:
         pltpu.make_async_remote_copy(
-            bbuf, bb.at[:, zh], b_send, b_recv, device_id={"ctx": cousin((zh + j) % n_blocks)}, device_id_type=MESH
+            bbuf, bb.at[:, zh], b_send, b_recv, device_id={"ctx": index}, device_id_type=MESH
         ).start()
     pltpu.make_async_copy(bb, bb, b_recv).wait()
 
@@ -435,10 +434,9 @@
 
     own_c = pltpu.make_async_copy(cbuf.at[pos], cr.at[pos], c_recv)
     own_c.start()
-    for j in range(1, group):
-        p = (pos + j) % group
+    for p, index in peers:
         pltpu.make_async_remote_copy(
-            cbuf.at[p], cr.at[pos], c_send, c_recv, device_id={"ctx": member(p)}, device_id_type=MESH
+            cbuf.at[p], cr.at[pos], c_send, c_recv, device_id={"ctx": index}, device_id_type=MESH
         ).start()
 
     for rim in rims[1:]:
@@ -455,6 +453,27 @@
     ahead_f = [[ahead_feat(i, k) for k in range(2)] for i in range(3)]
     ahead_gf = [ahead[3][k : k + 1] * ahead_f[0][k] for k in range(2)]
     ahead_gq = [ahead[3][k : k + 1] * ahead[4][k : k + 1] for k in range(2)]
+
+    gather = jnp.where(col == RUNS * lax.rem(row, run) + lax.div(row, run), 1.0, 0.0).astype(BF16)
+    last = lax.broadcasted_iota(jnp.int32, (RUNS, width), 0) == RUNS - 1
+
+    def finish(i, beyond):
+        for k in range(2):
+            head = pltpu.roll(gs[i, RUNS * k : RUNS * (k + 1), :], RUNS - 1, axis=0)
+            gs[i, rows + RUNS * k : rows + RUNS * (k + 1), :] = jnp.where(last, beyond[k], head)
+        made = (
+            tap(i, 0) * gs[i, :rows, :]
+            + tap(i, 1) * gs[i, RUNS : rows + RUNS, :]
+            + tap(i, 2) * gs[i, 2 * RUNS : rows + 2 * RUNS, :]
+        )
+        gp_ref[i] = jnp.dot(gather, made.astype(BF16), preferred_element_type=F32).astype(BF16)
+
+    gs[0, :rows, :] = gq[...]
+    finish(0, ahead_gq)
+    for m in range(MODES):
+        sloc[m] = coefs[m] * sloc[m]
+        coefs[m] = coefs[m] * jnp.exp(lams[m] * (float(run) * (rank - float(RUNS - 1))))
+        lams[m] = jnp.exp(-lams[m])
 
     pltpu.make_async_copy(cr, cr, c_recv).wait()
     flat[...] = cr[...].astype(F32).reshape(group * ROWS, half)
@@ -477,15 +496,10 @@
             gshort_ref[i, j : j + 1, :] = scale * (x_tot[3 + k : 4 + k, :] + total(item3(3 + k)))
     gskip_ref[...] = scale * x_tot[9:10, :]
 
-    rank_h = lax.broadcasted_iota(jnp.int32, (RUNS, half), 0).astype(F32)
     for h in range(2):
         lanes = slice(h * half, (h + 1) * half)
-        a, p = [], []
-        for m in range(MODES):
-            lam = lams[m, :, lanes]
-            back = jnp.exp(lam * (float(run) * (rank_h - float(RUNS - 1))))
-            a.append(jnp.exp(-lam))
-            p.append(coefs[m, :, lanes] * (sloc[m, :, lanes] + back * s_dev[m : m + 1, lanes]))
+        a = [lams[m, :, lanes] for m in range(MODES)]
+        p = [sloc[m, :, lanes] + coefs[m, :, lanes] * s_dev[m : m + 1, lanes] for m in range(MODES)]
         for r in range(run - 1, -1, -1):
             at = slice(RUNS * r, RUNS * (r + 1))
             p = [x * d for x, d in zip(p, a)]
@@ -495,28 +509,15 @@
             longs[at, lanes] += terms[0]
 
     gated = longs[...] + skip * gf[...]
-    gs[0, :rows, :] = gq[...]
     gs[1, :rows, :] = gated * feat[1]
     gs[2, :rows, :] = gated * feat[0]
     ahead_long = [
         total(coef_t * s_dev),
         total(coef_t * (s_dev - ahead_gf[0]) * jnp.exp(lam_t)),
     ]
-    last = lax.broadcasted_iota(jnp.int32, (RUNS, width), 0) == RUNS - 1
-    for k in range(2):
-        ahead_gated = (ahead_long[k] + skip * ahead_gf[k]) * has_after
-        beyond = (ahead_gq[k], ahead_gated * ahead_f[2][k], ahead_gated * ahead_f[1][k])
-        for i in range(3):
-            head = pltpu.roll(gs[i, RUNS * k : RUNS * (k + 1), :], RUNS - 1, axis=0)
-            gs[i, rows + RUNS * k : rows + RUNS * (k + 1), :] = jnp.where(last, beyond[i], head)
-    gather = jnp.where(col == RUNS * (row % run) + row // run, 1.0, 0.0).astype(BF16)
-    for i in range(3):
-        made = (
-            tap(i, 0) * gs[i, :rows, :]
-            + tap(i, 1) * gs[i, RUNS : rows + RUNS, :]
-            + tap(i, 2) * gs[i, 2 * RUNS : rows + 2 * RUNS, :]
-        )
-        gp_ref[i] = jnp.dot(gather, made.astype(BF16), preferred_element_type=F32).astype(BF16)
+    ahead_gated = [(ahead_long[k] + skip * ahead_gf[k]) * has_after for k in range(2)]
+    finish(1, [ahead_gated[k] * ahead_f[2][k] for k in range(2)])
+    finish(2, [ahead_gated[k] * ahead_f[1][k] for k in range(2)])
 
     for rim in rims:
         rim.wait_send()
@@ -565,6 +566,7 @@
             + [
                 pltpu.VMEM((3, rows + 16, width), F32),
                 pltpu.VMEM((2,) + full, F32),
+                pltpu.VMEM(full, F32),
                 pltpu.VMEM(full, F32),
                 pltpu.VMEM(full, F32),
                 pltpu.VMEM(full, F32),

time: 42.2 us -> 41.5 us (0.983)
  Pallas kernels: 41.4 us -> 40.7 us
    pallas_call x1, Pallas kernels: 40.6 us -> 39.9 us  [body(): pl.pallas_call(functools.partial(kernel, (n_ctx, n_blocks)), out_shape=[p...]
where the time goes in v3:
time: 41.5 us; the launch traced here: 41.3 us
  Pallas kernels  40.7 us (98%)
  between operations  0.64 us (2%)
    pallas_call x1, Pallas kernels, body(): pl.pallas_call(functools.partial(kernel, (n_ctx, n_blocks)), out_shape=[p...  39.9 us

profile of v3, /device:TPU:1, one launch (start us, length us, event | category | flops | bytes accessed | tf_op | source)
XLA Modules:
  0.0 41.3 jit_solution(18223584589959291828)
XLA Ops:
  0.6 39.9 %shard_map.110 = (bf16[3,256,256]{2,1,0:T(8,128)(2,1)S(1)}, f32[3,3,256]{2,1,0:T(4,128)S(1)}, f32[16,256]{1,0:T(8,128)S(1)}, f32[16,256]{1,0:T(8,128)S(1)}, f32[1,256]{1,0:T(1,128)S(1)}) custom-call(bf16[3,256,256]{2,1,0:T(8,128)(2,1)} %proj_hbm.1, bf16[256,256]{1,0:T(8,128)(2,1)} %filt_hbm.1, bf16[256,256]{1,0:T(8,128)(2,1)} %cot_hbm.1, ...), custom_call_target="tpu_custom_call" | custom-call | tf_op jit(solution)/shard_map/pallas_call | solution.py:560
  40.5 0.8 %shard_map.111 = (bf16[3,256,256]{2,1,0:T(8,128)(2,1)}, f32[3,3,256]{2,1,0:T(4,128)}, f32[16,256]{1,0:T(8,128)}, f32[16,256]{1,0:T(8,128)}, f32[1,256]{1,0:T(1,128)}) custom-call(bf16[3,256,256]{2,1,0:T(8,128)(2,1)S(1)} %get-tuple-element.15.refs_0_, f32[3,3,256]{2,1,0:T(4,128)S(1)} %get-tuple-element.16.refs_1_, f32[16,256]{1,0:T(8,128)S(1)} %get-tuple-element.17.refs_2_, ...), custom_call_target="tpu_custom_call" | custom-call | tf_op jit(solution)/shard_map/pallas_call | solution.py:608

commit v4 on v3

--- a/solution.py
+++ b/solution.py
@@ -15,6 +15,7 @@
 RUNS = 8
 MODES = 16
 ROWS = 16
+EARLY = 12
 ROW_L, ROW_LP, ROW_V, ROW_VP, ROW_W, ROW_R, ROW_D, ROW_X = 0, 1, 2, 3, 4, 10, 11, 12
 REST = 3
 
@@ -95,6 +96,7 @@
     cbuf,
     cr,
     gs,
+    rim_rows,
     halo_prev,
     halo_next,
     in_sem,
@@ -203,22 +205,6 @@
         ys[j] = masked(feat[1] * shifted(1, j))
         ys[3 + j] = masked(feat[0] * shifted(2, j))
 
-    pl.semaphore_wait(barrier, group - 1 + n_blocks - 1 + 2)
-    last_rows, first_rows = pl.ds(rows - 16, 16), pl.ds(0, 16)
-    rims = (
-        (proj_ref.at[:, last_rows], halo_prev, after),
-        (proj_ref.at[:, first_rows], halo_next.at[pl.ds(0, 3)], before),
-        (cot_ref.at[first_rows], halo_next.at[3], before),
-        (filt_ref.at[first_rows], halo_next.at[4], before),
-    )
-    rims = [
-        pltpu.make_async_remote_copy(
-            src, dst, halo_send.at[i], halo_recv.at[i], device_id={"ctx": to}, device_id_type=MESH
-        )
-        for i, (src, dst, to) in enumerate(rims)
-    ]
-    for rim in rims:
-        rim.start()
     longs[...] = jnp.zeros_like(longs)
     crosses[...] = jnp.zeros_like(crosses)
 
@@ -263,7 +249,31 @@
         put(ROW_D, total(d_sum + vp * s_loc + v * sp_loc))
         return 0
 
-    lax.fori_loop(0, MODES, one_mode, 0)
+    for i in range(3):
+        for b in range(2):
+            at = 16 + RUNS * (run - 1 - b) + RUNS - 1
+            rim_rows[2 * i + 1 - b : 2 * i + 2 - b, :] = ext[i, at : at + 1, :]
+    rim_rows[6:8, :] = jnp.zeros((2, width), F32)
+
+    lax.fori_loop(0, EARLY, one_mode, 0)
+
+    pl.semaphore_wait(barrier, group - 1 + n_blocks - 1 + 2)
+    first_rows = pl.ds(0, 16)
+    rims = (
+        (rim_rows, halo_prev, after),
+        (proj_ref.at[:, first_rows], halo_next.at[pl.ds(0, 3)], before),
+        (cot_ref.at[first_rows], halo_next.at[3], before),
+        (filt_ref.at[first_rows], halo_next.at[4], before),
+    )
+    rims = [
+        pltpu.make_async_remote_copy(
+            src, dst, halo_send.at[i], halo_recv.at[i], device_id={"ctx": to}, device_id_type=MESH
+        )
+        for i, (src, dst, to) in enumerate(rims)
+    ]
+    for rim in rims:
+        rim.start()
+    lax.fori_loop(EARLY, MODES, one_mode, 0)
 
     skip = skip_ref[...]
     inner_gated = longs[...] + skip * gf[...]
@@ -272,37 +282,40 @@
     plain += [total(inner_gated * ys[k]) + total(crosses[k]) for k in range(6)]
     plain.append(total(gf[...] * gv[...]))
 
+    def each_mode(k):
+        return jnp.concatenate(
+            [sums[(h * ROWS + k) * MODES : (h * ROWS + k + 1) * MODES, :] for h in range(2)], axis=1
+        )
+
+    def keep(k, value):
+        for h in range(2):
+            sums[(h * ROWS + k) * MODES : (h * ROWS + k + 1) * MODES, :] = value[:, h * half : (h + 1) * half]
+
+    a_t = jnp.exp(-lam_t)
+    back_two = jnp.exp(2.0 * lam_t)
+    two, two_slope = each_mode(ROW_L), each_mode(ROW_LP)
+    two, two_slope = back_two * two, back_two * (two_slope - 2.0 * two)
+    slope_1 = a_t * (two_slope + two)
+    moved = a_t * two
+    decays = [jnp.exp(lam_t * -float(rows)), jnp.exp(lam_t * -float(rows - 1))]
+    direct_sum, moved_sum = total(coef_t), total(coef_t * a_t)
+    cot_two = [cot[0:1], cot[RUNS : RUNS + 1]]
+
     rims[0].wait_recv()
     has_before = jnp.where(me > 0, 1.0, 0.0)
-    before_rows = [halo_prev[i].astype(F32)[14:16] * has_before for i in range(3)]
+    before_rows = [halo_prev[2 * i : 2 * i + 2, :] * has_before for i in range(3)]
     x = [
         {-2: before_rows[i][0:1], -1: before_rows[i][1:2], 0: ext[i, 16:17, :], 1: ext[i, 24:25, :]}
         for i in range(3)
     ]
     f = [[tap(i, 0) * x[i][t] + tap(i, 1) * x[i][t - 1] + tap(i, 2) * x[i][t - 2] for t in range(2)] for i in range(3)]
-    cot_two = [cot[0:1], cot[RUNS : RUNS + 1]]
     gf_two = [cot_two[t] * f[0][t] for t in range(2)]
     gv_two = [f[1][t] * f[2][t] for t in range(2)]
     ys_two = [[f[2][t] * x[1][t - j] for j in range(3)] + [f[1][t] * x[2][t - j] for j in range(3)] for t in range(2)]
 
-    def each_mode(k):
-        return jnp.concatenate(
-            [sums[(h * ROWS + k) * MODES : (h * ROWS + k + 1) * MODES, :] for h in range(2)], axis=1
-        )
-
-    def keep(k, value):
-        for h in range(2):
-            sums[(h * ROWS + k) * MODES : (h * ROWS + k + 1) * MODES, :] = value[:, h * half : (h + 1) * half]
-
-    a_t = jnp.exp(-lam_t)
-    back_two = jnp.exp(2.0 * lam_t)
-    two, two_slope = each_mode(ROW_L), each_mode(ROW_LP)
-    two, two_slope = back_two * two, back_two * (two_slope - 2.0 * two)
-    slope_1 = a_t * (two_slope + two)
-    state_1 = gf_two[1] + a_t * two
+    state_1 = gf_two[1] + moved
     slope_0 = a_t * (slope_1 + state_1)
     state_0 = gf_two[0] + a_t * state_1
-    decays = [jnp.exp(lam_t * -float(rows)), jnp.exp(lam_t * -float(rows - 1))]
     parts = [decays[t] * gv_two[t] for t in range(2)]
     keep(ROW_L, state_0)
     keep(ROW_LP, slope_0)
@@ -337,7 +350,7 @@
             sbuf.at[p], rbuf.at[pos], a_send, a_recv, device_id={"ctx": index}, device_id_type=MESH
         ).start()
 
-    direct = [total(coef_t) * gf_two[0] + total(coef_t * a_t) * gf_two[1], total(coef_t) * gf_two[1]]
+    direct = [direct_sum * gf_two[0] + moved_sum * gf_two[1], direct_sum * gf_two[1]]
     for t in range(2):
         at = slice(RUNS * t, RUNS * t + 1)
         gf[at, :] = gf_two[t]
@@ -589,7 +602,8 @@
                 pltpu.VMEM((32, ROWS, half), BF16),
                 pltpu.VMEM((32, ROWS, half), BF16),
                 pltpu.VMEM((3, rows + 16, width), F32),
-                pltpu.VMEM((3, 16, width), BF16),
+                pltpu.VMEM((8, width), F32),
+                pltpu.VMEM((8, width), F32),
                 pltpu.VMEM((5, 16, width), BF16),
                 pltpu.SemaphoreType.DMA((7,)),
                 pltpu.SemaphoreType.DMA((4,)),

time: 41.5 us -> 38.5 us (0.928)
  Pallas kernels: 40.7 us -> 37.7 us
    pallas_call x1, Pallas kernels: 39.9 us -> 36.9 us  [body(): pl.pallas_call(functools.partial(kernel, (n_ctx, n_blocks)), out_shape=[p...]
where the time goes in v4:
time: 38.5 us; the launch traced here: 38.3 us
  Pallas kernels  37.7 us (98%)
  between operations  0.64 us (2%)
    pallas_call x1, Pallas kernels, body(): pl.pallas_call(functools.partial(kernel, (n_ctx, n_blocks)), out_shape=[p...  36.9 us
    pallas_call x1, Pallas kernels, body(): pl.pallas_call(hand_over, out_shape=[pltpu.HBM(x.shape, x.dtype) for x in...  0.8 us

profile of v4, /device:TPU:1, one launch (start us, length us, event | category | flops | bytes accessed | tf_op | source)
XLA Modules:
  0.0 38.3 jit_solution(10246500675583867486)
XLA Ops:
  0.6 36.9 %shard_map.110 = (bf16[3,256,256]{2,1,0:T(8,128)(2,1)S(1)}, f32[3,3,256]{2,1,0:T(4,128)S(1)}, f32[16,256]{1,0:T(8,128)S(1)}, f32[16,256]{1,0:T(8,128)S(1)}, f32[1,256]{1,0:T(1,128)S(1)}) custom-call(bf16[3,256,256]{2,1,0:T(8,128)(2,1)} %proj_hbm.1, bf16[256,256]{1,0:T(8,128)(2,1)} %filt_hbm.1, bf16[256,256]{1,0:T(8,128)(2,1)} %cot_hbm.1, ...), custom_call_target="tpu_custom_call" | custom-call | tf_op jit(solution)/shard_map/pallas_call | solution.py:573
  37.5 0.8 %shard_map.111 = (bf16[3,256,256]{2,1,0:T(8,128)(2,1)}, f32[3,3,256]{2,1,0:T(4,128)}, f32[16,256]{1,0:T(8,128)}, f32[16,256]{1,0:T(8,128)}, f32[1,256]{1,0:T(1,128)}) custom-call(bf16[3,256,256]{2,1,0:T(8,128)(2,1)S(1)} %get-tuple-element.15.refs_0_, f32[3,3,256]{2,1,0:T(4,128)S(1)} %get-tuple-element.16.refs_1_, f32[16,256]{1,0:T(8,128)S(1)} %get-tuple-element.17.refs_2_, ...), custom_call_target="tpu_custom_call" | custom-call | tf_op jit(solution)/shard_map/pallas_call | solution.py:622

commit v5 on v4

--- a/solution.py
+++ b/solution.py
@@ -16,6 +16,7 @@
 MODES = 16
 ROWS = 16
 EARLY = 12
+TOGETHER = 2
 ROW_L, ROW_LP, ROW_V, ROW_VP, ROW_W, ROW_R, ROW_D, ROW_X = 0, 1, 2, 3, 4, 10, 11, 12
 REST = 3
 
@@ -99,6 +100,7 @@
     rim_rows,
     halo_prev,
     halo_next,
+    passed_on,
     in_sem,
     halo_send,
     halo_recv,
@@ -147,7 +149,7 @@
     cousins = [y * (per_block * n_blocks) + lax.rem(zh + j, n_blocks) * per_block + lo for j in (2, 1, 3)]
     before, after = lax.rem(me + n_ctx - 1, n_ctx), lax.rem(me + 1, n_ctx)
     barrier = pltpu.get_barrier_semaphore()
-    for d in cousins + [index for _, index in peers] + [before, after]:
+    for d in [index for _, index in peers] + cousins[1:] + [before, after]:
         pl.semaphore_signal(barrier, inc=1, device_id={"ctx": d}, device_id_type=MESH)
 
     row = lax.broadcasted_iota(jnp.int32, (rows, rows), 0)
@@ -210,44 +212,57 @@
 
     rank = lax.broadcasted_iota(jnp.int32, (RUNS, width), 0).astype(F32)
 
-    def one_mode(m, _):
-        lam = lams[m]
-        coef = coefs[m]
-        a = jnp.exp(-lam)
-        zero = jnp.zeros((RUNS, width), F32)
-        state, slope, r_sum, d_sum, vp = zero, zero, zero, zero, zero
-        w = [zero] * 6
+    def some_modes(at, _):
+        for h in range(2):
+            some_modes_of_half(at, h)
+        return 0
+
+    def some_modes_of_half(at, h):
+        lanes = slice(h * half, (h + 1) * half)
+        modes = [at * TOGETHER + i for i in range(TOGETHER)]
+        lam = [lams[m, :, lanes] for m in modes]
+        coef = [coefs[m, :, lanes] for m in modes]
+        a = [jnp.exp(-x) for x in lam]
+        zero = jnp.zeros((RUNS, half), F32)
+        state, slope, r_sum, d_sum, vp = ([zero] * TOGETHER for _ in range(5))
+        w = [[zero] * 6 for _ in modes]
         for step in range(run):
             low = slice(RUNS * (run - 1 - step), RUNS * (run - step))
             high = slice(RUNS * step, RUNS * (step + 1))
-            slope = a * (slope + state)
-            state = a * state + gf[low, :]
-            longs[low, :] += coef * state
-            gv_low = gv[low, :]
-            r_sum = r_sum + gv_low * state
-            d_sum = d_sum + gv_low * slope
-            vp = a * (vp + gz[high, :])
+            gf_low, gv_low, gz_high = gf[low, lanes], gv[low, lanes], gz[high, lanes]
+            ys_high = [ys[k, high, lanes] for k in range(6)]
+            part = None
+            for i in range(TOGETHER):
+                slope[i] = a[i] * (slope[i] + state[i])
+                state[i] = a[i] * state[i] + gf_low
+                given = coef[i] * state[i]
+                part = given if part is None else part + given
+                r_sum[i] = r_sum[i] + gv_low * state[i]
+                d_sum[i] = d_sum[i] + gv_low * slope[i]
+                vp[i] = a[i] * (vp[i] + gz_high)
+                for k in range(6):
+                    w[i][k] = a[i] * (w[i][k] + ys_high[k])
+            longs[low, lanes] += part
+        rank_h = rank[:, lanes]
+        for i, m in enumerate(modes):
+            v = sum(taps_ref[1, j : j + 1, lanes] * w[i][j] for j in range(3))
+            inner, inner_slope, s_loc, sp_loc = suffix(state[i], slope[i], lam[i], run, RUNS)
+            sloc[m, :, lanes] = s_loc
+            weight = jnp.exp(lam[i] * (float(run) * (rank_h - float(RUNS - 1))))
+
+            def put(k, value):
+                sums[pl.ds((h * ROWS + k) * MODES + m, 1), :] = value
+
+            put(ROW_L, inner[0:1, :])
+            put(ROW_LP, inner_slope[0:1, :])
+            put(ROW_V, total(weight * v))
+            put(ROW_VP, total(weight * (vp[i] + float(run) * (float(RUNS - 1) - rank_h) * v)))
+            state_in = coef[i] * s_loc
             for k in range(6):
-                w[k] = a * (w[k] + ys[k, high, :])
-        v = tap(1, 0) * w[0] + tap(1, 1) * w[1] + tap(1, 2) * w[2]
-        inner, inner_slope, s_loc, sp_loc = suffix(state, slope, lam, run, RUNS)
-        sloc[m] = s_loc
-        weight = jnp.exp(lam * (float(run) * (rank - float(RUNS - 1))))
-        def put(k, value):
-            for h in range(2):
-                sums[pl.ds((h * ROWS + k) * MODES + m, 1), :] = value[:, h * half : (h + 1) * half]
-
-        put(ROW_L, inner[0:1, :])
-        put(ROW_LP, inner_slope[0:1, :])
-        put(ROW_V, total(weight * v))
-        put(ROW_VP, total(weight * (vp + float(run) * (float(RUNS - 1) - rank) * v)))
-        state_in = coef * s_loc
-        for k in range(6):
-            put(ROW_W + k, total(weight * w[k]))
-            crosses[k] += state_in * w[k]
-        put(ROW_R, total(r_sum + v * s_loc))
-        put(ROW_D, total(d_sum + vp * s_loc + v * sp_loc))
-        return 0
+                put(ROW_W + k, total(weight * w[i][k]))
+                crosses[k, :, lanes] += state_in * w[i][k]
+            put(ROW_R, total(r_sum[i] + v * s_loc))
+            put(ROW_D, total(d_sum[i] + vp[i] * s_loc + v * sp_loc))
 
     for i in range(3):
         for b in range(2):
@@ -255,9 +270,11 @@
             rim_rows[2 * i + 1 - b : 2 * i + 2 - b, :] = ext[i, at : at + 1, :]
     rim_rows[6:8, :] = jnp.zeros((2, width), F32)
 
-    lax.fori_loop(0, EARLY, one_mode, 0)
-
-    pl.semaphore_wait(barrier, group - 1 + n_blocks - 1 + 2)
+    lax.fori_loop(0, EARLY // TOGETHER, some_modes, 0)
+
+    pl.semaphore_wait(barrier, group - 1 + 2 + 2)
+    for d in cousins[1:]:
+        pl.semaphore_signal(passed_on, inc=1, device_id={"ctx": d}, device_id_type=MESH)
     first_rows = pl.ds(0, 16)
     rims = (
         (rim_rows, halo_prev, after),
@@ -273,7 +290,7 @@
     ]
     for rim in rims:
         rim.start()
-    lax.fori_loop(EARLY, MODES, one_mode, 0)
+    lax.fori_loop(EARLY // TOGETHER, MODES // TOGETHER, some_modes, 0)
 
     skip = skip_ref[...]
     inner_gated = longs[...] + skip * gf[...]
@@ -405,6 +422,7 @@
 
     own_b = pltpu.make_async_copy(bbuf, bb.at[:, zh], b_recv)
     own_b.start()
+    pl.semaphore_wait(passed_on, 2)
     for index in cousins:
         pltpu.make_async_remote_copy(
             bbuf, bb.at[:, zh], b_send, b_recv, device_id={"ctx": index}, device_id_type=MESH
@@ -605,6 +623,7 @@
                 pltpu.VMEM((8, width), F32),
                 pltpu.VMEM((8, width), F32),
                 pltpu.VMEM((5, 16, width), BF16),
+                pltpu.SemaphoreType.REGULAR,
                 pltpu.SemaphoreType.DMA((7,)),
                 pltpu.SemaphoreType.DMA((4,)),
                 pltpu.SemaphoreType.DMA((4,)),

time: 38.5 us -> 38.1 us (0.990)
  Pallas kernels: 37.7 us -> 37.3 us
    pallas_call x1, Pallas kernels: 36.9 us -> 36.5 us  [body(): pl.pallas_call(functools.partial(kernel, (n_ctx, n_blocks)), out_shape=[p...]
where the time goes in v5:
time: 38.1 us; the launch traced here: 37.9 us
  Pallas kernels  37.3 us (98%)
  between operations  0.64 us (2%)
    pallas_call x1, Pallas kernels, body(): pl.pallas_call(functools.partial(kernel, (n_ctx, n_blocks)), out_shape=[p...  36.5 us
    pallas_call x1, Pallas kernels, body(): pl.pallas_call(hand_over, out_shape=[pltpu.HBM(x.shape, x.dtype) for x in...  0.8 us

profile of v5, /device:TPU:1, one launch (start us, length us, event | category | flops | bytes accessed | tf_op | source)
XLA Modules:
  0.0 37.9 jit_solution(2929340881463592402)
XLA Ops:
  0.6 36.5 %shard_map.110 = (bf16[3,256,256]{2,1,0:T(8,128)(2,1)S(1)}, f32[3,3,256]{2,1,0:T(4,128)S(1)}, f32[16,256]{1,0:T(8,128)S(1)}, f32[16,256]{1,0:T(8,128)S(1)}, f32[1,256]{1,0:T(1,128)S(1)}) custom-call(bf16[3,256,256]{2,1,0:T(8,128)(2,1)} %proj_hbm.1, bf16[256,256]{1,0:T(8,128)(2,1)} %filt_hbm.1, bf16[256,256]{1,0:T(8,128)(2,1)} %cot_hbm.1, ...), custom_call_target="tpu_custom_call" | custom-call | tf_op jit(solution)/shard_map/pallas_call | solution.py:591
  37.1 0.8 %shard_map.111 = (bf16[3,256,256]{2,1,0:T(8,128)(2,1)}, f32[3,3,256]{2,1,0:T(4,128)}, f32[16,256]{1,0:T(8,128)}, f32[16,256]{1,0:T(8,128)}, f32[1,256]{1,0:T(1,128)}) custom-call(bf16[3,256,256]{2,1,0:T(8,128)(2,1)S(1)} %get-tuple-element.15.refs_0_, f32[3,3,256]{2,1,0:T(4,128)S(1)} %get-tuple-element.16.refs_1_, f32[16,256]{1,0:T(8,128)S(1)} %get-tuple-element.17.refs_2_, ...), custom_call_target="tpu_custom_call" | custom-call | tf_op jit(solution)/shard_map/pallas_call | solution.py:641

commit v6 on v5

--- a/solution.py
+++ b/solution.py
@@ -138,13 +138,16 @@
         load.start()
 
     ys_of = [lax.rem(y + d, 4) for d in range(4)]
-    los_of = [lo] + [lax.rem(lo + d, per_block) for d in range(1, per_block)]
     bases = [v * (per_block * n_blocks) + zh * per_block for v in ys_of]
+    zl, core = lax.div(lo, 2), lax.rem(lo, 2)
+    zls_of = (zl, zl + 1 - 2 * lax.rem(zl, 2), lax.rem(zl + 2, 4), 3 - zl)
+    los_of = [[2 * v + core, 2 * v + 1 - core] for v in zls_of]
+    steps = ((2, 3), (2, 2), (1, 3), (3, 3), (1, 2), (3, 2), (2, 1), (0, 3), (2, 0), (0, 2), (1, 1), (3, 1), (1, 0), (3, 0), (0, 1), (0, 0))
     peers = [
-        (ys_of[d] * per_block + los_of[k], bases[d] + los_of[k])
-        for d in (2, 1, 3, 0)
-        for k in (2, 6, 3, 5, 4, 7, 1, 0)
-        if (d, k) != (0, 0)
+        (ys_of[d] * per_block + los_of[k][c], bases[d] + los_of[k][c])
+        for d, k in steps
+        for c in (1, 0)
+        if (d, k, c) != (0, 0, 0)
     ]
     cousins = [y * (per_block * n_blocks) + lax.rem(zh + j, n_blocks) * per_block + lo for j in (2, 1, 3)]
     before, after = lax.rem(me + n_ctx - 1, n_ctx), lax.rem(me + 1, n_ctx)

time: 38.1 us -> 37.8 us (level)
  Pallas kernels: 37.3 us -> 36.9 us
where the time goes in v6:
time: 37.8 us; the launch traced here: 37.6 us
  Pallas kernels  36.9 us (98%)
  between operations  0.64 us (2%)
    pallas_call x1, Pallas kernels, body(): pl.pallas_call(functools.partial(kernel, (n_ctx, n_blocks)), out_shape=[p...  36.1 us
    pallas_call x1, Pallas kernels, body(): pl.pallas_call(hand_over, out_shape=[pltpu.HBM(x.shape, x.dtype) for x in...  0.8 us

profile of v6, /device:TPU:1, one launch (start us, length us, event | category | flops | bytes accessed | tf_op | source)
XLA Modules:
  0.0 37.6 jit_solution(5349153351788733652)
XLA Ops:
  0.6 36.1 %shard_map.110 = (bf16[3,256,256]{2,1,0:T(8,128)(2,1)S(1)}, f32[3,3,256]{2,1,0:T(4,128)S(1)}, f32[16,256]{1,0:T(8,128)S(1)}, f32[16,256]{1,0:T(8,128)S(1)}, f32[1,256]{1,0:T(1,128)S(1)}) custom-call(bf16[3,256,256]{2,1,0:T(8,128)(2,1)} %proj_hbm.1, bf16[256,256]{1,0:T(8,128)(2,1)} %filt_hbm.1, bf16[256,256]{1,0:T(8,128)(2,1)} %cot_hbm.1, ...), custom_call_target="tpu_custom_call" | custom-call | tf_op jit(solution)/shard_map/pallas_call | solution.py:594
  36.8 0.8 %shard_map.111 = (bf16[3,256,256]{2,1,0:T(8,128)(2,1)}, f32[3,3,256]{2,1,0:T(4,128)}, f32[16,256]{1,0:T(8,128)}, f32[16,256]{1,0:T(8,128)}, f32[1,256]{1,0:T(1,128)}) custom-call(bf16[3,256,256]{2,1,0:T(8,128)(2,1)S(1)} %get-tuple-element.15.refs_0_, f32[3,3,256]{2,1,0:T(4,128)S(1)} %get-tuple-element.16.refs_1_, f32[16,256]{1,0:T(8,128)S(1)} %get-tuple-element.17.refs_2_, ...), custom_call_target="tpu_custom_call" | custom-call | tf_op jit(solution)/shard_map/pallas_call | solution.py:644

commit v7 on v6

--- a/solution.py
+++ b/solution.py
@@ -564,10 +564,9 @@
 def hand_over(*refs):
     count = (len(refs) - 1) // 2
     sems = refs[-1]
-    copies = [
-        pltpu.make_async_copy(src, dst, sems.at[i])
-        for i, (src, dst) in enumerate(zip(refs[:count], refs[count : 2 * count]))
-    ]
+    pairs = [(refs[0].at[i], refs[count].at[i]) for i in range(3)]
+    pairs += list(zip(refs[1:count], refs[count + 1 : 2 * count]))
+    copies = [pltpu.make_async_copy(src, dst, sems.at[i]) for i, (src, dst) in enumerate(pairs)]
     for copy in copies:
         copy.start()
     for copy in copies:
@@ -646,7 +645,7 @@
             out_shape=[pltpu.HBM(x.shape, x.dtype) for x in made],
             in_specs=[vmem] * 5,
             out_specs=[pl.BlockSpec(memory_space=pltpu.HBM)] * 5,
-            scratch_shapes=[pltpu.SemaphoreType.DMA((5,))],
+            scratch_shapes=[pltpu.SemaphoreType.DMA((7,))],
         )(*(pltpu.with_memory_space_constraint(x, pltpu.VMEM) for x in out))
         return out[0], out[1], out[2].T, out[3].T, out[4].reshape(width)
 

time: 37.8 us -> 37.8 us (level)
  no operation moved by 1% of the time
where the time goes in v7:
time: 37.8 us; the launch traced here: 37.6 us
  Pallas kernels  37 us (98%)
  between operations  0.64 us (2%)
    pallas_call x1, Pallas kernels, body(): pl.pallas_call(functools.partial(kernel, (n_ctx, n_blocks)), out_shape=[p...  36.1 us
    pallas_call x1, Pallas kernels, body(): pl.pallas_call(hand_over, out_shape=[pltpu.HBM(x.shape, x.dtype) for x in...  0.81 us

profile of v7, /device:TPU:1, one launch (start us, length us, event | category | flops | bytes accessed | tf_op | source)
XLA Modules:
  0.0 37.6 jit_solution(18005887192862978193)
XLA Ops:
  0.6 36.1 %shard_map.110 = (bf16[3,256,256]{2,1,0:T(8,128)(2,1)S(1)}, f32[3,3,256]{2,1,0:T(4,128)S(1)}, f32[16,256]{1,0:T(8,128)S(1)}, f32[16,256]{1,0:T(8,128)S(1)}, f32[1,256]{1,0:T(1,128)S(1)}) custom-call(bf16[3,256,256]{2,1,0:T(8,128)(2,1)} %proj_hbm.1, bf16[256,256]{1,0:T(8,128)(2,1)} %filt_hbm.1, bf16[256,256]{1,0:T(8,128)(2,1)} %cot_hbm.1, ...), custom_call_target="tpu_custom_call" | custom-call | tf_op jit(solution)/shard_map/pallas_call | solution.py:593
  36.8 0.8 %shard_map.111 = (bf16[3,256,256]{2,1,0:T(8,128)(2,1)}, f32[3,3,256]{2,1,0:T(4,128)}, f32[16,256]{1,0:T(8,128)}, f32[16,256]{1,0:T(8,128)}, f32[1,256]{1,0:T(1,128)}) custom-call(bf16[3,256,256]{2,1,0:T(8,128)(2,1)S(1)} %get-tuple-element.15.refs_0_, f32[3,3,256]{2,1,0:T(4,128)S(1)} %get-tuple-element.16.refs_1_, f32[16,256]{1,0:T(8,128)S(1)} %get-tuple-element.17.refs_2_, ...), custom_call_target="tpu_custom_call" | custom-call | tf_op jit(solution)/shard_map/pallas_call | solution.py:643
